TPU v7x, 256 devices: a whole 4x4x8 slice. The times are simulated.
256 devices in a mesh: clip: 2 (over y_hi), blk: 16 (over x, y_lo, core), heads: 8 (over z).
Axes of the slice: x: 4, y: 4 (y_hi: 2, y_lo: 2; y = y_hi * 2 + y_lo), z: 8, core: 2. Of those that a mesh axis runs over, the one named last changes fastest.
Arguments:
- queries: bfloat16 [20480, 3072], P(('clip', 'blk', 'heads')), parts along dimension 0, may hold values from -9 to 9
- keys: bfloat16 [20480, 3072], P(('clip', 'blk', 'heads')), parts along dimension 0, may hold values from -9 to 9
- values: bfloat16 [20480, 3072], P(('clip', 'blk', 'heads')), parts along dimension 0, may hold values from -6 to 6
- out_weight: bfloat16 [3072, 5120], P('heads'), may hold values from -0.109375 to 0.109375
Outputs:
- projected: bfloat16 [20480, 5120], P(('clip', 'blk', 'heads')), parts along dimension 0
There are 2 independent parts, one for each index of `clip`. A program takes and returns all parts, laid end to end along the dimension named above; an argument that names none is the same for every part. Nothing has to cross between parts.
All inputs are finite; a program needn't handle non-finite values.
Results may differ from a plain program's by a relative error of at most 0.02.
Values may be sent and summed in bfloat16 or wider, within the bound.
No kernel may reach another device: no remote copies, remote signals or barrier semaphores. Data moves between devices by JAX's collectives and lax.ppermute only.
A program may use at most 128 MiB of HBM per device.

v0:
```python
import jax
import jax.numpy as jnp
import numpy as np
from jax import lax
from jax.experimental import pallas as pl
from jax.experimental.pallas import tpu as pltpu
from jax.sharding import Mesh
from jax.sharding import PartitionSpec as P

HDIM = 128
LOG2E = 1.4426950408889634
SCALE = HDIM**-0.5 * LOG2E
EXTRA = 32


def shift(block, axis, distance):
    n = lax.axis_size(axis)
    if distance % n == 0:
        return block
    return lax.ppermute(block, axis, [(i, (i + distance) % n) for i in range(n)])


def from_all(block, axis, wait=lambda value: value):
    behind, ahead = shift(block, axis, 1), shift(block, axis, -1)
    middle = block.shape[0] // 2
    onward, backward = wait(behind[:middle]), wait(ahead[middle:])
    return [(block,), (behind,), (ahead,), (shift(onward, axis, 1), shift(backward, axis, -1))]


def after(value, *done):
    return lax.optimization_barrier((value, *done))[0]


def params(mebibytes):
    return pltpu.CompilerParams(vmem_limit_bytes=mebibytes * 1024 * 1024)


def regroup_kernel(q_ref, k_ref, v_ref, queries_ref, pairs_ref):
    groups, heads = queries_ref.shape[:2]
    for g in range(groups):
        for h in range(heads):
            first = (g * heads + h) * HDIM
            queries_ref[g, h] = q_ref[:, first : first + HDIM]
            pairs_ref[g, 2 * h] = k_ref[:, first : first + HDIM]
            pairs_ref[g, 2 * h + 1] = v_ref[:, first : first + HDIM]


def regroup(queries, keys, values, groups):
    rows, full = queries.shape
    heads = full // groups // HDIM
    like = lambda n: jax.ShapeDtypeStruct((groups, n, rows, HDIM), queries.dtype)
    return pl.pallas_call(
        regroup_kernel,
        out_shape=[like(heads), like(2 * heads)],
        compiler_params=params(56),
    )(queries, keys, values)


def diagonal():
    shape = (HDIM, HDIM)
    return lax.broadcasted_iota(jnp.int32, shape, 0) == lax.broadcasted_iota(jnp.int32, shape, 1)


def attend_kernel(q_ref, *refs):
    *pair_refs, out_ref = refs
    groups, _, each, _ = q_ref.shape
    rows = groups * each
    q = q_ref[:, 0].reshape(rows, HDIM)
    tiles, held = [[]], 0
    for ref in pair_refs:
        if held == 2 * groups:
            tiles, held = tiles + [[]], 0
        tiles[-1].append(ref)
        held += ref.shape[0]

    def tile(i, which):
        parts = [ref[:, which].reshape(-1, HDIM) for ref in tiles[i]]
        return jnp.concatenate(parts, axis=0)

    def scores_of(i):
        return lax.dot_general(
            q, tile(i, 0), (((1,), (1,)), ((), ())), preferred_element_type=jnp.float32
        )

    highest, total = None, None
    scores = scores_of(0)
    for i in range(len(tiles)):
        later = scores_of(i + 1) if i + 1 < len(tiles) else None
        value = tile(i, 1)
        value = jnp.concatenate([value, jnp.ones_like(value)], axis=1)
        tile_max = jnp.max(scores, axis=1, keepdims=True)
        new = tile_max if highest is None else jnp.maximum(highest, tile_max)
        weights = jnp.exp2((scores - new) * SCALE).astype(jnp.bfloat16)
        part = jnp.dot(weights, value, preferred_element_type=jnp.float32)
        if highest is None:
            total = part
        else:
            total = total * jnp.exp2((highest - new) * SCALE) + part
        highest, scores = new, later
    sums = total[:, HDIM:]
    out_ref[0, :rows] = (total[:, :HDIM] / sums).astype(jnp.bfloat16)
    logs = highest * SCALE + jnp.log(sums) * LOG2E
    same, line = diagonal(), lax.broadcasted_iota(jnp.int32, (8, HDIM), 0)
    packed = jnp.zeros((8, HDIM), jnp.float32)
    for b in range(rows // HDIM):
        part = logs[b * HDIM : (b + 1) * HDIM]
        row = jnp.sum(jnp.where(same, part, 0.0), axis=0, keepdims=True)
        packed = jnp.where(line == b, row, packed)
    high = packed.astype(jnp.bfloat16).astype(jnp.float32)
    middle = (packed - high).astype(jnp.bfloat16).astype(jnp.float32)
    low = packed - high - middle
    out_ref[0, rows:] = jnp.concatenate(
        [high, middle, low, jnp.zeros_like(low)], axis=0
    ).astype(jnp.bfloat16)


def attend(queries, pairs):
    groups, heads, each, _ = queries.shape
    rows = groups * each
    pair = lambda a: pl.BlockSpec((a.shape[0], 2, each, HDIM), lambda h: (0, h, 0, 0))
    keys = sum(a.shape[0] for a in pairs) * each
    scores = heads * rows * keys
    return pl.pallas_call(
        attend_kernel,
        grid=(heads,),
        in_specs=[pl.BlockSpec((groups, 1, each, HDIM), lambda h: (0, h, 0, 0))]
        + [pair(a) for a in pairs],
        out_specs=pl.BlockSpec((1, rows + EXTRA, HDIM), lambda h: (h, 0, 0)),
        out_shape=jax.ShapeDtypeStruct((heads, rows + EXTRA, HDIM), jnp.bfloat16),
        compiler_params=params(48),
        cost_estimate=pl.CostEstimate(
            flops=scores * HDIM * 4 * 4,
            bytes_accessed=heads * keys * HDIM * 4,
            transcendentals=scores,
        ),
    )(queries, *pairs)


def merge_kernel(a_ref, b_ref, out_ref):
    groups, heads, rows, _ = out_ref.shape
    tokens = groups * rows
    same = diagonal()

    def logs(ref, h):
        extra = ref[h, tokens:].astype(jnp.float32)
        return extra[0:8] + extra[8:16] + extra[16:24]

    for h in range(heads):
        difference = logs(b_ref, h) - logs(a_ref, h)
        share = 1.0 / (1.0 + jnp.exp2(difference))
        columns = [
            jnp.sum(jnp.where(same, share[r : r + 1], 0.0), axis=1, keepdims=True)
            for r in range(tokens // HDIM)
        ]
        column = jnp.concatenate(columns, axis=0)
        for g in range(groups):
            part = slice(g * rows, (g + 1) * rows)
            a, b = a_ref[h, part].astype(jnp.float32), b_ref[h, part].astype(jnp.float32)
            out_ref[g, h] = (b + (a - b) * column[part]).astype(jnp.bfloat16)


def merge(a, b, groups):
    heads, tokens = a.shape[0], a.shape[1] - EXTRA
    shape = (groups, heads, tokens // groups, HDIM)
    return pl.pallas_call(
        merge_kernel,
        out_shape=jax.ShapeDtypeStruct(shape, jnp.bfloat16),
        compiler_params=params(16),
    )(a, b)


def project_kernel(c_ref, in_ref, near_ref, far_ref, out_ref, near, far):
    step = pl.program_id(0)
    groups, heads = in_ref.shape[:2]
    attention = jnp.concatenate(
        [in_ref[g, h] for g in range(groups) for h in range(heads)], axis=1
    )
    for weight_ref, total in ((near_ref, near), (far_ref, far)):
        part = jnp.dot(attention, weight_ref[...], preferred_element_type=jnp.float32)

        @pl.when(step == 0)
        def _(part=part, total=total):
            total[...] = part

        @pl.when(step > 0)
        def _(part=part, total=total):
            total[...] += part

    @pl.when(step == pl.num_programs(0) - 1)
    def _():
        columns = near.shape[1]
        for total, at in ((near, c_ref[0]), (far, 1 - c_ref[0])):
            place = pl.ds(pl.multiple_of(at * columns, HDIM), columns)
            out_ref[:, place] = total[...].astype(out_ref.dtype)


def project(c, attention, near, far):
    groups, heads, rows, _ = attention.shape
    depth, columns = near.shape
    steps = 4
    weight = pl.BlockSpec((depth // steps, columns), lambda i, c: (i, 0))
    return pl.pallas_call(
        project_kernel,
        grid_spec=pltpu.PrefetchScalarGridSpec(
            num_scalar_prefetch=1,
            grid=(steps,),
            in_specs=[
                pl.BlockSpec((groups // steps, heads, rows, HDIM), lambda i, c: (i, 0, 0, 0)),
                weight,
                weight,
            ],
            out_specs=pl.BlockSpec((rows, 2 * columns), lambda i, c: (0, 0)),
            scratch_shapes=[pltpu.VMEM((rows, columns), jnp.float32)] * 2,
        ),
        out_shape=jax.ShapeDtypeStruct((rows, 2 * columns), jnp.bfloat16),
        compiler_params=params(16),
        cost_estimate=pl.CostEstimate(
            flops=4 * rows * depth * columns, bytes_accessed=depth * columns * 4, transcendentals=0
        ),
    )(c, attention, near, far)


def place_kernel(x_ref, *refs):
    *in_refs, out_ref = refs
    columns = in_refs[0].shape[1]
    for i, ref in enumerate(in_refs):
        at = lax.rem(x_ref[0] + i, len(in_refs)) * columns
        out_ref[:, pl.ds(pl.multiple_of(at, HDIM), columns)] = ref[...]


def place(x, pieces):
    rows, columns = pieces[0].shape
    whole = pl.BlockSpec((rows, columns), lambda i, x: (0, 0))
    return pl.pallas_call(
        place_kernel,
        grid_spec=pltpu.PrefetchScalarGridSpec(
            num_scalar_prefetch=1,
            grid=(1,),
            in_specs=[whole] * len(pieces),
            out_specs=pl.BlockSpec((rows, len(pieces) * columns), lambda i, x: (0, 0)),
        ),
        out_shape=jax.ShapeDtypeStruct((rows, len(pieces) * columns), pieces[0].dtype),
        compiler_params=params(16),
    )(x, *pieces)


def per_device(queries, keys, values, out_weight):
    groups, across = lax.axis_size("z"), lax.axis_size("x")
    x, c = lax.axis_index("x"), lax.axis_index("c")

    grouped, grouped_pairs = regroup(queries, keys, values, groups)
    pairs = lax.all_to_all(grouped_pairs, "z", 0, 0, tiled=True)
    moved = from_all(pairs, "x")
    q = lax.all_to_all(after(grouped, pairs), "z", 0, 0, tiled=True)
    q_beside = shift(after(q, *moved[1], *moved[2]), "y", 1)

    columns = out_weight.shape[1] // across
    half = columns // 2
    mine = lax.dynamic_slice_in_dim(after(out_weight, pairs), x * columns + c * half, half, axis=1)
    weight = lax.all_gather(mine, "z", axis=0, tiled=True)

    all_pairs = [part for piece in moved for part in (*piece, *(shift(p, "c", 1) for p in piece))]
    partial_beside = attend(q_beside, all_pairs)
    partial = attend(after(q, partial_beside), all_pairs)
    attention = merge(partial, shift(partial_beside, "y", 1), groups)

    back = lax.all_to_all(attention, "z", 0, 0, tiled=True)
    weight_beside = shift(after(weight, attention), "c", 1)
    place_c = c.astype(jnp.int32)[None]
    last = project(place_c, back, weight, weight_beside)
    returned = [last]
    there = from_all(back, "x", lambda value: after(value, last))
    for (piece, *rest), distance in zip(there[1:], (1, -1, 2)):
        piece = jnp.concatenate([piece, *rest], axis=0) if rest else piece
        last = project(place_c, after(piece, last), weight, weight_beside)
        returned.append(shift(last, "x", -distance))
    own, ahead, behind, over = returned
    return place(x.astype(jnp.int32)[None], [own, ahead, over, behind])


def solution(mesh):
    clip, blk, z = mesh.devices.shape
    devices = np.array(mesh.devices).reshape(clip, blk // 4, 2, 2, z)
    tokens = ("clip", "x", "y", "c", "z")
    return jax.shard_map(
        per_device,
        mesh=Mesh(devices, tokens),
        in_specs=(P(tokens, None), P(tokens, None), P(tokens, None), P("z", None)),
        out_specs=P(tokens, None),
        check_vma=False,
    )
```

profile of v0, /device:TPU:16, one launch (start us, length us, event | category | flops | bytes accessed | tf_op | source)
XLA Modules:
  0.0 190.5 jit_solution(1346615680718023416)
XLA Ops:
  6.5 2.7 %shard_map.46 = (bf16[8,3,80,128]{3,2,1,0:T(8,128)(2,1)}, bf16[8,6,80,128]{3,2,1,0:T(8,128)(2,1)}) custom-call(bf16[80,3072]{1,0:T(8,128)(2,1)} %q_ref.1, bf16[80,3072]{1,0:T(8,128)(2,1)} %k_ref.1, bf16[80,3072]{1,0:T(8,128)(2,1)} %v_ref.1), custom_call_target="tpu_custom_call" | custom-call | tf_op jit(solution)/shard_map/pallas_call | solution.py:52
  9.2 8.5 %all-to-all-start = ((bf16[8,6,80,128]{3,2,1,0:T(8,128)(2,1)}), bf16[8,6,80,128]{3,2,1,0:T(8,128)(2,1)S(1)}, u32[]{:S(2)}, u32[]{:S(2)}) async-start(bf16[8,6,80,128]{3,2,1,0:T(8,128)(2,1)} %get-tuple-element.18), calls=%async_computation | async-start | bytes 1966080 | tf_op jit(solution)/shard_map/all_to_all | solution.py:252
  17.8 27.3 %all-to-all-done.refs_0_ = bf16[8,6,80,128]{3,2,1,0:T(8,128)(2,1)S(1)} async-done(((bf16[8,6,80,128]{3,2,1,0:T(8,128)(2,1)}), bf16[8,6,80,128]{3,2,1,0:T(8,128)(2,1)S(1)}, u32[]{:S(2)}, u32[]{:S(2)}) %all-to-all-start) | async-done | bytes 983072 | tf_op jit(solution)/shard_map/all_to_all | solution.py:252
  45.0 1.8 constant_dynamic-slice_fusion
  50.2 3.5 %all-to-all-start.1 = ((bf16[8,3,80,128]{3,2,1,0:T(8,128)(2,1)}), bf16[8,3,80,128]{3,2,1,0:T(8,128)(2,1)S(1)}, u32[]{:S(2)}, u32[]{:S(2)}) async-start(bf16[8,3,80,128]{3,2,1,0:T(8,128)(2,1)} %get-tuple-element.19), calls=%async_computation.1 | async-start | bytes 983040 | tf_op jit(solution)/shard_map/all_to_all | solution.py:254
  53.7 18.2 %collective-permute-done.refs_2_ = bf16[8,6,80,128]{3,2,1,0:T(8,128)(2,1)S(1)} collective-permute-done((bf16[8,6,80,128]{3,2,1,0:T(8,128)(2,1)S(1)}, bf16[8,6,80,128]{3,2,1,0:T(8,128)(2,1)S(1)}, u32[]{:S(2)}, u32[]{:S(2)}) %collective-permute-start) | collective-permute-done | bytes 983072 | tf_op jit(solution)/shard_map/ppermute | solution.py:20
  73.0 1.9 slice.17
  74.9 3.0 %collective-permute-start.7 = (bf16[4,6,80,128]{3,2,1,0:T(8,128)(2,1)}, bf16[4,6,80,128]{3,2,1,0:T(8,128)(2,1)}, u32[]{:S(2)}, u32[]{:S(2)}) collective-permute-start(bf16[4,6,80,128]{3,2,1,0:T(8,128)(2,1)} %slice.17), channel_id=1, source_target_pairs={{0,96},{32,0},{64,32},{96,64},{1,97},{33,1},{65,33},{97,65},{2,98}... | collective-permute-start | bytes 1474568 | tf_op jit(solution)/shard_map/ppermute | solution.py:20
  79.6 7.0 %collective-permute-done.6.refs_6_ = bf16[4,6,80,128]{3,2,1,0:T(8,128)(2,1)} collective-permute-done((bf16[4,6,80,128]{3,2,1,0:T(8,128)(2,1)}, bf16[4,6,80,128]{3,2,1,0:T(8,128)(2,1)}, u32[]{:S(2)}, u32[]{:S(2)}) %collective-permute-start.6) | collective-permute-done | bytes 491552 | tf_op jit(solution)/shard_map/ppermute | solution.py:20
  87.8 3.8 %collective-permute-done.2.q_ref = bf16[8,3,80,128]{3,2,1,0:T(8,128)(2,1)S(1)} collective-permute-done((bf16[8,3,80,128]{3,2,1,0:T(8,128)(2,1)S(1)}, bf16[8,3,80,128]{3,2,1,0:T(8,128)(2,1)S(1)}, u32[]{:S(2)}, u32[]{:S(2)}) %collective-permute-start.2) | collective-permute-done | bytes 491552 | tf_op jit(solution)/shard_map/ppermute | solution.py:20
  91.6 13.7 %shard_map.47 = bf16[3,672,128]{2,1,0:T(8,128)(2,1)S(1)} custom-call(bf16[8,3,80,128]{3,2,1,0:T(8,128)(2,1)S(1)} %collective-permute-done.2.q_ref, bf16[8,6,80,128]{3,2,1,0:T(8,128)(2,1)S(1)} %all-to-all-done.refs_0_, bf16[8,6,80,128]{3,2,1,0:T(8,128)(2,1)S(1)} %collective-permute-done.3.refs_1_, bf16[8,6,80,128]{3,2,1,0:T(8,128)(2,1)S(1)} %collective-permute-done.refs_2_, ...), custom_call_target="tpu_custom_call" | custom-call | flops 20132659200 | bytes 7864320 | tf_op jit(solution)/shard_map/pallas_call | solution.py:123
  106.9 13.7 %shard_map.48.a_ref = bf16[3,672,128]{2,1,0:T(8,128)(2,1)S(1)} custom-call(bf16[8,3,80,128]{3,2,1,0:T(8,128)(2,1)S(1)} %all-to-all-done.1.q_ref, bf16[8,6,80,128]{3,2,1,0:T(8,128)(2,1)S(1)} %all-to-all-done.refs_0_, bf16[8,6,80,128]{3,2,1,0:T(8,128)(2,1)S(1)} %collective-permute-done.3.refs_1_, bf16[8,6,80,128]{3,2,1,0:T(8,128)(2,1)S(1)} %collective-permute-done.refs_2_, ...), custom_call_target="tpu_custom_call" | custom-call | flops 20132659200 | bytes 7864320 | tf_op jit(solution)/shard_map/pallas_call | solution.py:123
  121.3 20.1 %all_to_all.15.in_ref = bf16[8,3,80,128]{3,2,1,0:T(8,128)(2,1)S(1)} all-to-all(bf16[8,3,80,128]{3,2,1,0:T(8,128)(2,1)S(1)} %shard_map.49), channel_id=1, replica_groups=mesh['clip'=2,'x'=4,'y'=2,'c'=2,'z'=8] {'z'}, dimensions={0} | all-to-all | bytes 983040 | tf_op jit(solution)/shard_map/all_to_all | solution.py:267
  141.5 3.2 %collective-permute-start.15 = (bf16[8,3,80,128]{3,2,1,0:T(8,128)(2,1)S(1)}, bf16[8,3,80,128]{3,2,1,0:T(8,128)(2,1)S(1)}, u32[]{:S(2)}, u32[]{:S(2)}) collective-permute-start(bf16[8,3,80,128]{3,2,1,0:T(8,128)(2,1)S(1)} %all_to_all.15.in_ref), channel_id=1, source_target_pairs={{0,96},{32,0},{64,32},{96,64},{1,97},{33,1},{65,33},{97,65},{2,98}... | collective-permute-start | bytes 1474568 | tf_op jit(solution)/shard_map/ppermute | solution.py:20
  144.7 11.2 %collective-permute-done.12.in_ref = bf16[8,3,80,128]{3,2,1,0:T(8,128)(2,1)S(1)} collective-permute-done((bf16[8,3,80,128]{3,2,1,0:T(8,128)(2,1)S(1)}, bf16[8,3,80,128]{3,2,1,0:T(8,128)(2,1)S(1)}, u32[]{:S(2)}, u32[]{:S(2)}) %collective-permute-start.12) | collective-permute-done | bytes 491552 | tf_op jit(solution)/shard_map/ppermute | solution.py:20
  155.9 2.1 %copy-done = bf16[3072,640]{1,0:T(8,128)(2,1)S(1)} copy-done((bf16[3072,640]{1,0:T(8,128)(2,1)S(1)}, bf16[3072,640]{1,0:T(8,128)(2,1)}, u32[]{:S(2)}) %copy-start) | copy-done | bytes 3932184
  158.1 2.7 %shard_map.50.refs_0_ = bf16[80,1280]{1,0:T(8,128)(2,1)S(1)} custom-call(s32[1]{0:T(128)} %bitcast.1.c_ref, bf16[8,3,80,128]{3,2,1,0:T(8,128)(2,1)S(1)} %all_to_all.15.in_ref, bf16[3072,640]{1,0:T(8,128)(2,1)S(1)} %copy-done, bf16[3072,640]{1,0:T(8,128)(2,1)S(1)} %collective-permute-done.11.far_ref), custom_call_target="tpu_custom_call" | custom-call | flops 629145600 | bytes 7864320 | tf_op jit(solution)/shard_map/pallas_call | solution.py:202
  161.0 3.1 %collective-permute-start.16 = (bf16[4,3,80,128]{3,2,1,0:T(8,128)(2,1)S(1)}, bf16[4,3,80,128]{3,2,1,0:T(8,128)(2,1)S(1)}, u32[]{:S(2)}, u32[]{:S(2)}) collective-permute-start(bf16[4,3,80,128]{3,2,1,0:T(8,128)(2,1)S(1)} %slice.19), channel_id=1, source_target_pairs={{0,96},{32,0},{64,32},{96,64},{1,97},{33,1},{65,33},{97,65},{2,98}... | collective-permute-start | bytes 737288 | tf_op jit(solution)/shard_map/ppermute | solution.py:20
  164.1 2.7 %shard_map.51 = bf16[80,1280]{1,0:T(8,128)(2,1)S(1)} custom-call(s32[1]{0:T(128)} %bitcast.1.c_ref, bf16[8,3,80,128]{3,2,1,0:T(8,128)(2,1)S(1)} %collective-permute-done.12.in_ref, bf16[3072,640]{1,0:T(8,128)(2,1)S(1)} %copy-done, bf16[3072,640]{1,0:T(8,128)(2,1)S(1)} %collective-permute-done.11.far_ref), custom_call_target="tpu_custom_call" | custom-call | flops 629145600 | bytes 7864320 | tf_op jit(solution)/shard_map/pallas_call | solution.py:202
  166.8 1.8 collective-permute-start.13
  168.6 2.7 %shard_map.52 = bf16[80,1280]{1,0:T(8,128)(2,1)S(1)} custom-call(s32[1]{0:T(128)} %bitcast.1.c_ref, bf16[8,3,80,128]{3,2,1,0:T(8,128)(2,1)S(1)} %collective-permute-done.15.in_ref, bf16[3072,640]{1,0:T(8,128)(2,1)S(1)} %copy-done, bf16[3072,640]{1,0:T(8,128)(2,1)S(1)} %collective-permute-done.11.far_ref), custom_call_target="tpu_custom_call" | custom-call | flops 629145600 | bytes 7864320 | tf_op jit(solution)/shard_map/pallas_call | solution.py:202
  171.7 2.7 %shard_map.53 = bf16[80,1280]{1,0:T(8,128)(2,1)S(1)} custom-call(s32[1]{0:T(128)} %bitcast.1.c_ref, bf16[8,3,80,128]{3,2,1,0:T(8,128)(2,1)S(1)} %pad_maximum_fusion.in_ref, bf16[3072,640]{1,0:T(8,128)(2,1)S(1)} %copy-done, bf16[3072,640]{1,0:T(8,128)(2,1)S(1)} %collective-permute-done.11.far_ref), custom_call_target="tpu_custom_call" | custom-call | flops 629145600 | bytes 7864320 | tf_op jit(solution)/shard_map/pallas_call | solution.py:202
  174.5 2.3 %collective-permute-start.17 = (bf16[80,1280]{1,0:T(8,128)(2,1)S(1)}, bf16[80,1280]{1,0:T(8,128)(2,1)S(1)}, u32[]{:S(2)}, u32[]{:S(2)}) collective-permute-start(bf16[80,1280]{1,0:T(8,128)(2,1)S(1)} %shard_map.53), channel_id=1, source_target_pairs={{0,64},{32,96},{64,0},{96,32},{1,65},{33,97},{65,1},{97,33},{2,66}... | collective-permute-start | bytes 614408 | tf_op jit(solution)/shard_map/ppermute | solution.py:20
  176.8 5.9 %collective-permute-done.18.refs_3_ = bf16[80,1280]{1,0:T(8,128)(2,1)S(1)} collective-permute-done((bf16[80,1280]{1,0:T(8,128)(2,1)S(1)}, bf16[80,1280]{1,0:T(8,128)(2,1)S(1)}, u32[]{:S(2)}, u32[]{:S(2)}) %collective-permute-start.18) | collective-permute-done | bytes 204832 | tf_op jit(solution)/shard_map/ppermute | solution.py:20
  (39 shorter events, 11.4 us)
Async XLA Ops:
  9.2 35.8 %all-to-all-start = ((bf16[8,6,80,128]{3,2,1,0:T(8,128)(2,1)}), bf16[8,6,80,128]{3,2,1,0:T(8,128)(2,1)S(1)}, u32[]{:S(2)}, u32[]{:S(2)}) async-start(bf16[8,6,80,128]{3,2,1,0:T(8,128)(2,1)} %get-tuple-element.18), calls=%async_computation | async-start | bytes 1966080 | tf_op jit(solution)/shard_map/all_to_all | solution.py:252
  17.7 103.5 %all-gather.2.cloned.1.call-start = ((), (), s32[]{:S(2)}) async-start(), calls=%async_computation.3 | async-start | bytes 4423680 | tf_op jit(solution)/shard_map/all_gather | solution.py:260
  46.9 25.0 %collective-permute-start = (bf16[8,6,80,128]{3,2,1,0:T(8,128)(2,1)S(1)}, bf16[8,6,80,128]{3,2,1,0:T(8,128)(2,1)S(1)}, u32[]{:S(2)}, u32[]{:S(2)}) collective-permute-start(bf16[8,6,80,128]{3,2,1,0:T(8,128)(2,1)S(1)} %all-to-all-done.refs_0_), channel_id=1, source_target_pairs={{0,32},{32,64},{64,96},{96,0},{1,33},{33,65},{65,97},{97,1},{2,34}... | collective-permute-start | bytes 2949128 | tf_op jit(solution)/shard_map/ppermute | solution.py:20
  48.5 24.6 %collective-permute-start.1 = (bf16[8,6,80,128]{3,2,1,0:T(8,128)(2,1)S(1)}, bf16[8,6,80,128]{3,2,1,0:T(8,128)(2,1)}, u32[]{:S(2)}, u32[]{:S(2)}) collective-permute-start(bf16[8,6,80,128]{3,2,1,0:T(8,128)(2,1)S(1)} %all-to-all-done.refs_0_), channel_id=1, source_target_pairs={{0,96},{32,0},{64,32},{96,64},{1,97},{33,1},{65,33},{97,65},{2,98}... | collective-permute-start | bytes 2949128 | tf_op jit(solution)/shard_map/ppermute | solution.py:20
  50.2 28.1 %collective-permute-start.3 = (bf16[8,6,80,128]{3,2,1,0:T(8,128)(2,1)S(1)}, bf16[8,6,80,128]{3,2,1,0:T(8,128)(2,1)S(1)}, u32[]{:S(2)}, u32[]{:S(2)}) collective-permute-start(bf16[8,6,80,128]{3,2,1,0:T(8,128)(2,1)S(1)} %all-to-all-done.refs_0_), channel_id=1, source_target_pairs={{0,8},{8,0},{1,9},{9,1},{2,10},{10,2},{3,11},{11,3},{4,12},{12,4},... | collective-permute-start | bytes 2949128 | tf_op jit(solution)/shard_map/ppermute | solution.py:20
  50.2 28.1 %all-to-all-start.1 = ((bf16[8,3,80,128]{3,2,1,0:T(8,128)(2,1)}), bf16[8,3,80,128]{3,2,1,0:T(8,128)(2,1)S(1)}, u32[]{:S(2)}, u32[]{:S(2)}) async-start(bf16[8,3,80,128]{3,2,1,0:T(8,128)(2,1)} %get-tuple-element.19), calls=%async_computation.1 | async-start | bytes 983040 | tf_op jit(solution)/shard_map/all_to_all | solution.py:254
  72.7 13.9 %collective-permute-start.6 = (bf16[4,6,80,128]{3,2,1,0:T(8,128)(2,1)}, bf16[4,6,80,128]{3,2,1,0:T(8,128)(2,1)}, u32[]{:S(2)}, u32[]{:S(2)}) collective-permute-start(bf16[4,6,80,128]{3,2,1,0:T(8,128)(2,1)} %slice.16), channel_id=1, source_target_pairs={{0,32},{32,64},{64,96},{96,0},{1,33},{33,65},{65,97},{97,1},{2,34}... | collective-permute-start | bytes 1474568 | tf_op jit(solution)/shard_map/ppermute | solution.py:20
  74.9 12.9 %collective-permute-start.7 = (bf16[4,6,80,128]{3,2,1,0:T(8,128)(2,1)}, bf16[4,6,80,128]{3,2,1,0:T(8,128)(2,1)}, u32[]{:S(2)}, u32[]{:S(2)}) collective-permute-start(bf16[4,6,80,128]{3,2,1,0:T(8,128)(2,1)} %slice.17), channel_id=1, source_target_pairs={{0,96},{32,0},{64,32},{96,64},{1,97},{33,1},{65,33},{97,65},{2,98}... | collective-permute-start | bytes 1474568 | tf_op jit(solution)/shard_map/ppermute | solution.py:20
  77.8 13.7 %collective-permute-start.4 = (bf16[8,6,80,128]{3,2,1,0:T(8,128)(2,1)S(1)}, bf16[8,6,80,128]{3,2,1,0:T(8,128)(2,1)}, u32[]{:S(2)}, u32[]{:S(2)}) collective-permute-start(bf16[8,6,80,128]{3,2,1,0:T(8,128)(2,1)S(1)} %collective-permute-done.refs_2_), channel_id=1, source_target_pairs={{0,8},{8,0},{1,9},{9,1},{2,10},{10,2},{3,11},{11,3},{4,12},{12,4},... | collective-permute-start | bytes 2949128 | tf_op jit(solution)/shard_map/ppermute | solution.py:20
  77.9 13.7 %collective-permute-start.5 = (bf16[8,6,80,128]{3,2,1,0:T(8,128)(2,1)}, bf16[8,6,80,128]{3,2,1,0:T(8,128)(2,1)}, u32[]{:S(2)}, u32[]{:S(2)}) collective-permute-start(bf16[8,6,80,128]{3,2,1,0:T(8,128)(2,1)} %collective-permute-done.1.refs_4_), channel_id=1, source_target_pairs={{0,8},{8,0},{1,9},{9,1},{2,10},{10,2},{3,11},{11,3},{4,12},{12,4},... | collective-permute-start | bytes 2949128 | tf_op jit(solution)/shard_map/ppermute | solution.py:20
  78.4 13.2 %collective-permute-start.2 = (bf16[8,3,80,128]{3,2,1,0:T(8,128)(2,1)S(1)}, bf16[8,3,80,128]{3,2,1,0:T(8,128)(2,1)S(1)}, u32[]{:S(2)}, u32[]{:S(2)}) collective-permute-start(bf16[8,3,80,128]{3,2,1,0:T(8,128)(2,1)S(1)} %all-to-all-done.1.q_ref), channel_id=1, source_target_pairs={{0,16},{16,0},{1,17},{17,1},{2,18},{18,2},{3,19},{19,3},{4,20},{20... | collective-permute-start | bytes 1474568 | tf_op jit(solution)/shard_map/ppermute | solution.py:20
  86.7 4.9 %collective-permute-start.8 = (bf16[4,6,80,128]{3,2,1,0:T(8,128)(2,1)}, bf16[4,6,80,128]{3,2,1,0:T(8,128)(2,1)S(1)}, u32[]{:S(2)}, u32[]{:S(2)}) collective-permute-start(bf16[4,6,80,128]{3,2,1,0:T(8,128)(2,1)} %collective-permute-done.6.refs_6_), channel_id=1, source_target_pairs={{0,8},{8,0},{1,9},{9,1},{2,10},{10,2},{3,11},{11,3},{4,12},{12,4},... | collective-permute-start | bytes 1474568 | tf_op jit(solution)/shard_map/ppermute | solution.py:20
  87.8 3.8 %collective-permute-start.9 = (bf16[4,6,80,128]{3,2,1,0:T(8,128)(2,1)}, bf16[4,6,80,128]{3,2,1,0:T(8,128)(2,1)S(1)}, u32[]{:S(2)}, u32[]{:S(2)}) collective-permute-start(bf16[4,6,80,128]{3,2,1,0:T(8,128)(2,1)} %collective-permute-done.7.refs_7_), channel_id=1, source_target_pairs={{0,8},{8,0},{1,9},{9,1},{2,10},{10,2},{3,11},{11,3},{4,12},{12,4},... | collective-permute-start | bytes 1474568 | tf_op jit(solution)/shard_map/ppermute | solution.py:20
  105.3 15.2 %collective-permute-start.10 = (bf16[3,672,128]{2,1,0:T(8,128)(2,1)S(1)}, bf16[3,672,128]{2,1,0:T(8,128)(2,1)S(1)}, u32[]{:S(2)}, u32[]{:S(2)}) collective-permute-start(bf16[3,672,128]{2,1,0:T(8,128)(2,1)S(1)} %shard_map.47), channel_id=1, source_target_pairs={{0,16},{16,0},{1,17},{17,1},{2,18},{18,2},{3,19},{19,3},{4,20},{20... | collective-permute-start | bytes 1548296 | tf_op jit(solution)/shard_map/ppermute | solution.py:20
  121.2 34.7 %collective-permute-start.11 = (bf16[3072,640]{1,0:T(8,128)(2,1)}, bf16[3072,640]{1,0:T(8,128)(2,1)S(1)}, u32[]{:S(2)}, u32[]{:S(2)}) collective-permute-start(bf16[3072,640]{1,0:T(8,128)(2,1)} %all-gather.2.cloned.1.call-done.near_ref), channel_id=1, source_target_pairs={{0,8},{8,0},{1,9},{9,1},{2,10},{10,2},{3,11},{11,3},{4,12},{12,4},... | collective-permute-start | bytes 11796488 | tf_op jit(solution)/shard_map/ppermute | solution.py:20
  141.5 14.4 %collective-permute-start.12 = (bf16[8,3,80,128]{3,2,1,0:T(8,128)(2,1)S(1)}, bf16[8,3,80,128]{3,2,1,0:T(8,128)(2,1)S(1)}, u32[]{:S(2)}, u32[]{:S(2)}) collective-permute-start(bf16[8,3,80,128]{3,2,1,0:T(8,128)(2,1)S(1)} %all_to_all.15.in_ref), channel_id=1, source_target_pairs={{0,32},{32,64},{64,96},{96,0},{1,33},{33,65},{65,97},{97,1},{2,34}... | collective-permute-start | bytes 1474568 | tf_op jit(solution)/shard_map/ppermute | solution.py:20
  141.5 14.4 %collective-permute-start.15 = (bf16[8,3,80,128]{3,2,1,0:T(8,128)(2,1)S(1)}, bf16[8,3,80,128]{3,2,1,0:T(8,128)(2,1)S(1)}, u32[]{:S(2)}, u32[]{:S(2)}) collective-permute-start(bf16[8,3,80,128]{3,2,1,0:T(8,128)(2,1)S(1)} %all_to_all.15.in_ref), channel_id=1, source_target_pairs={{0,96},{32,0},{64,32},{96,64},{1,97},{33,1},{65,33},{97,65},{2,98}... | collective-permute-start | bytes 1474568 | tf_op jit(solution)/shard_map/ppermute | solution.py:20
  155.9 2.1 %copy-start = (bf16[3072,640]{1,0:T(8,128)(2,1)S(1)}, bf16[3072,640]{1,0:T(8,128)(2,1)}, u32[]{:S(2)}) copy-start(bf16[3072,640]{1,0:T(8,128)(2,1)} %all-gather.2.cloned.1.call-done.near_ref) | copy-start | bytes 11796484
  160.8 10.9 %collective-permute-start.14 = (bf16[4,3,80,128]{3,2,1,0:T(8,128)(2,1)S(1)}, bf16[4,3,80,128]{3,2,1,0:T(8,128)(2,1)S(1)}, u32[]{:S(2)}, u32[]{:S(2)}) collective-permute-start(bf16[4,3,80,128]{3,2,1,0:T(8,128)(2,1)S(1)} %slice.18), channel_id=1, source_target_pairs={{0,32},{32,64},{64,96},{96,0},{1,33},{33,65},{65,97},{97,1},{2,34}... | collective-permute-start | bytes 737288 | tf_op jit(solution)/shard_map/ppermute | solution.py:20
  161.0 10.7 %collective-permute-start.16 = (bf16[4,3,80,128]{3,2,1,0:T(8,128)(2,1)S(1)}, bf16[4,3,80,128]{3,2,1,0:T(8,128)(2,1)S(1)}, u32[]{:S(2)}, u32[]{:S(2)}) collective-permute-start(bf16[4,3,80,128]{3,2,1,0:T(8,128)(2,1)S(1)} %slice.19), channel_id=1, source_target_pairs={{0,96},{32,0},{64,32},{96,64},{1,97},{33,1},{65,33},{97,65},{2,98}... | collective-permute-start | bytes 737288 | tf_op jit(solution)/shard_map/ppermute | solution.py:20
  166.8 15.9 %collective-permute-start.13 = (bf16[80,1280]{1,0:T(8,128)(2,1)S(1)}, bf16[80,1280]{1,0:T(8,128)(2,1)S(1)}, u32[]{:S(2)}, u32[]{:S(2)}) collective-permute-start(bf16[80,1280]{1,0:T(8,128)(2,1)S(1)} %shard_map.51), channel_id=1, source_target_pairs={{0,96},{32,0},{64,32},{96,64},{1,97},{33,1},{65,33},{97,65},{2,98}... | collective-permute-start | bytes 614408 | tf_op jit(solution)/shard_map/ppermute | solution.py:20
  171.3 11.4 %collective-permute-start.18 = (bf16[80,1280]{1,0:T(8,128)(2,1)S(1)}, bf16[80,1280]{1,0:T(8,128)(2,1)S(1)}, u32[]{:S(2)}, u32[]{:S(2)}) collective-permute-start(bf16[80,1280]{1,0:T(8,128)(2,1)S(1)} %shard_map.52), channel_id=1, source_target_pairs={{0,32},{32,64},{64,96},{96,0},{1,33},{33,65},{65,97},{97,1},{2,34}... | collective-permute-start | bytes 614408 | tf_op jit(solution)/shard_map/ppermute | solution.py:20
  174.5 8.3 %collective-permute-start.17 = (bf16[80,1280]{1,0:T(8,128)(2,1)S(1)}, bf16[80,1280]{1,0:T(8,128)(2,1)S(1)}, u32[]{:S(2)}, u32[]{:S(2)}) collective-permute-start(bf16[80,1280]{1,0:T(8,128)(2,1)S(1)} %shard_map.53), channel_id=1, source_target_pairs={{0,64},{32,96},{64,0},{96,32},{1,65},{33,97},{65,1},{97,33},{2,66}... | collective-permute-start | bytes 614408 | tf_op jit(solution)/shard_map/ppermute | solution.py:20
Sparse Core Ops, SparseCore 0:
  47.0 59.0 all-gather.1
where the time goes:
time: 191 us
  waiting for transfers between devices  74.5 us (39%)
  Pallas kernels  42.6 us (22%)
  starting transfers between devices  33 us (17%)
  blocking collectives  20.1 us (11%)
  between operations  13.6 us (7%)
  local copies, waits for them, and re-layouts  6.72 us (4%)
    ppermute x19, waiting for transfers between devices, shift(): lax.ppermute(block, axis, [(i, (i + distance) % n) for i in range(n)])  47.2 us
    pallas_call x2, Pallas kernels, attend(): pl.pallas_call(attend_kernel, grid=(heads,), in_specs=[pl.BlockSpec((grou...  27.4 us
    all_to_all x1, waiting for transfers between devices, per_device(): pairs = lax.all_to_all(grouped_pairs, 'z', 0, 0, tiled=True)  27.3 us
    ppermute x19, starting transfers between devices, shift(): lax.ppermute(block, axis, [(i, (i + distance) % n) for i in range(n)])  21 us
    all_to_all x1, blocking collectives, per_device(): back = lax.all_to_all(attention, 'z', 0, 0, tiled=True)  20.1 us
    pallas_call x4, Pallas kernels, project(): pl.pallas_call(project_kernel, grid_spec=pltpu.PrefetchScalarGridSpec(num...  10.8 us
    all_to_all x1, starting transfers between devices, per_device(): pairs = lax.all_to_all(grouped_pairs, 'z', 0, 0, tiled=True)  8.47 us
  transfers between devices with their start and end apart: 22, of which 7 were waited for; matrix products, arithmetic and copies ran while one was open for 1% of the time, Pallas kernels for 19%

commit v1 on v0

--- a/solution.py
+++ b/solution.py
@@ -1,3 +1,5 @@
+import functools
+
 import jax
 import jax.numpy as jnp
 import numpy as np
@@ -20,11 +22,19 @@
     return lax.ppermute(block, axis, [(i, (i + distance) % n) for i in range(n)])
 
 
-def from_all(block, axis, wait=lambda value: value):
+def ring(block, axis):
+    middle = block.shape[0] // 2
+    low, high = block[:middle], block[middle:]
+    behind_low, ahead_high = shift(low, axis, 1), shift(high, axis, -1)
+    behind_high, ahead_low = shift(high, axis, 1), shift(low, axis, -1)
+    across = [shift(behind_low, axis, 1), shift(ahead_high, axis, -1)]
+    return [block], [behind_low, behind_high], [ahead_low, ahead_high], across
+
+
+def two_steps(block, axis):
     behind, ahead = shift(block, axis, 1), shift(block, axis, -1)
     middle = block.shape[0] // 2
-    onward, backward = wait(behind[:middle]), wait(ahead[middle:])
-    return [(block,), (behind,), (ahead,), (shift(onward, axis, 1), shift(backward, axis, -1))]
+    return [block], [behind], [ahead], [shift(behind[:middle], axis, 1), shift(ahead[middle:], axis, -1)]
 
 
 def after(value, *done):
@@ -35,25 +45,38 @@
     return pltpu.CompilerParams(vmem_limit_bytes=mebibytes * 1024 * 1024)
 
 
-def regroup_kernel(q_ref, k_ref, v_ref, queries_ref, pairs_ref):
+def regroup_kernel(at_ref, q_ref, k_ref, v_ref, weight_ref, queries_ref, pairs_ref, columns_ref):
     groups, heads = queries_ref.shape[:2]
     for g in range(groups):
         for h in range(heads):
-            first = (g * heads + h) * HDIM
-            queries_ref[g, h] = q_ref[:, first : first + HDIM]
-            pairs_ref[g, 2 * h] = k_ref[:, first : first + HDIM]
-            pairs_ref[g, 2 * h + 1] = v_ref[:, first : first + HDIM]
-
-
-def regroup(queries, keys, values, groups):
+            part = slice((g * heads + h) * HDIM, (g * heads + h + 1) * HDIM)
+            queries_ref[g, h] = q_ref[:, part]
+            pairs_ref[g, 2 * h] = k_ref[:, part]
+            pairs_ref[g, 2 * h + 1] = v_ref[:, part]
+    columns_ref[...] = weight_ref[...]
+
+
+def regroup(at, queries, keys, values, out_weight, columns, groups):
     rows, full = queries.shape
     heads = full // groups // HDIM
-    like = lambda n: jax.ShapeDtypeStruct((groups, n, rows, HDIM), queries.dtype)
+    block = pl.BlockSpec((out_weight.shape[0], columns), lambda i, at: (0, at[0]))
+    whole = lambda a: pl.BlockSpec(a.shape, lambda i, at: (0,) * len(a.shape))
+    shapes = [
+        jax.ShapeDtypeStruct((groups, heads, rows, HDIM), queries.dtype),
+        jax.ShapeDtypeStruct((groups, 2 * heads, rows, HDIM), queries.dtype),
+        jax.ShapeDtypeStruct((out_weight.shape[0], columns), out_weight.dtype),
+    ]
     return pl.pallas_call(
         regroup_kernel,
-        out_shape=[like(heads), like(2 * heads)],
+        grid_spec=pltpu.PrefetchScalarGridSpec(
+            num_scalar_prefetch=1,
+            grid=(1,),
+            in_specs=[whole(queries)] * 3 + [block],
+            out_specs=[whole(a) for a in shapes],
+        ),
+        out_shape=shapes,
         compiler_params=params(56),
-    )(queries, keys, values)
+    )(at, queries, keys, values, out_weight)
 
 
 def diagonal():
@@ -169,11 +192,15 @@
     )(a, b)
 
 
-def project_kernel(c_ref, in_ref, near_ref, far_ref, out_ref, near, far):
-    step = pl.program_id(0)
-    groups, heads = in_ref.shape[:2]
+def project_kernel(c_ref, *refs, pieces):
+    low_refs, high_refs = refs[:pieces], refs[pieces : 2 * pieces]
+    near_ref, far_ref, *out_refs, near, far = refs[2 * pieces :]
+    step, steps = pl.program_id(0), pl.num_programs(0)
+    groups, heads, rows, _ = low_refs[0].shape
+    flat = lambda ref: jnp.concatenate([ref[g, h] for g in range(groups) for h in range(heads)], axis=1)
     attention = jnp.concatenate(
-        [in_ref[g, h] for g in range(groups) for h in range(heads)], axis=1
+        [jnp.where(step < steps // 2, flat(low), flat(high)) for low, high in zip(low_refs, high_refs)],
+        axis=0,
     )
     for weight_ref, total in ((near_ref, near), (far_ref, far)):
         part = jnp.dot(attention, weight_ref[...], preferred_element_type=jnp.float32)
@@ -186,38 +213,39 @@
         def _(part=part, total=total):
             total[...] += part
 
-    @pl.when(step == pl.num_programs(0) - 1)
+    @pl.when(step == steps - 1)
     def _():
         columns = near.shape[1]
         for total, at in ((near, c_ref[0]), (far, 1 - c_ref[0])):
             place = pl.ds(pl.multiple_of(at * columns, HDIM), columns)
-            out_ref[:, place] = total[...].astype(out_ref.dtype)
-
-
-def project(c, attention, near, far):
-    groups, heads, rows, _ = attention.shape
+            for p, out_ref in enumerate(out_refs):
+                out_ref[:, place] = total[p * rows : (p + 1) * rows].astype(out_ref.dtype)
+
+
+def project(c, pieces, near, far):
     depth, columns = near.shape
     steps = 4
+    lows, highs = [piece[0] for piece in pieces], [piece[-1] for piece in pieces]
+    _, heads, rows, _ = lows[0].shape
+    groups = depth // heads // HDIM // steps
+    first = 0 if len(pieces[0]) == 2 else steps // 2
+    part = (groups, heads, rows, HDIM)
+    low = pl.BlockSpec(part, lambda i, c: (jnp.minimum(i, steps // 2 - 1), 0, 0, 0))
+    high = pl.BlockSpec(part, lambda i, c: (jnp.maximum(i - steps // 2, 0) + first, 0, 0, 0))
     weight = pl.BlockSpec((depth // steps, columns), lambda i, c: (i, 0))
-    return pl.pallas_call(
-        project_kernel,
+    out = jax.ShapeDtypeStruct((rows, 2 * columns), jnp.bfloat16)
+    return pl.pallas_call(
+        functools.partial(project_kernel, pieces=len(pieces)),
         grid_spec=pltpu.PrefetchScalarGridSpec(
             num_scalar_prefetch=1,
             grid=(steps,),
-            in_specs=[
-                pl.BlockSpec((groups // steps, heads, rows, HDIM), lambda i, c: (i, 0, 0, 0)),
-                weight,
-                weight,
-            ],
-            out_specs=pl.BlockSpec((rows, 2 * columns), lambda i, c: (0, 0)),
-            scratch_shapes=[pltpu.VMEM((rows, columns), jnp.float32)] * 2,
+            in_specs=[low] * len(pieces) + [high] * len(pieces) + [weight, weight],
+            out_specs=[pl.BlockSpec(out.shape, lambda i, c: (0, 0))] * len(pieces),
+            scratch_shapes=[pltpu.VMEM((len(pieces) * rows, columns), jnp.float32)] * 2,
         ),
-        out_shape=jax.ShapeDtypeStruct((rows, 2 * columns), jnp.bfloat16),
+        out_shape=[out] * len(pieces),
         compiler_params=params(16),
-        cost_estimate=pl.CostEstimate(
-            flops=4 * rows * depth * columns, bytes_accessed=depth * columns * 4, transcendentals=0
-        ),
-    )(c, attention, near, far)
+    )(c, *lows, *highs, near, far)
 
 
 def place_kernel(x_ref, *refs):
@@ -246,36 +274,31 @@
 
 def per_device(queries, keys, values, out_weight):
     groups, across = lax.axis_size("z"), lax.axis_size("x")
-    x, c = lax.axis_index("x"), lax.axis_index("c")
-
-    grouped, grouped_pairs = regroup(queries, keys, values, groups)
-    pairs = lax.all_to_all(grouped_pairs, "z", 0, 0, tiled=True)
-    moved = from_all(pairs, "x")
+    x, c = (lax.axis_index(axis).astype(jnp.int32)[None] for axis in ("x", "c"))
+    half = out_weight.shape[1] // across // 2
+
+    grouped, pairs, columns = regroup(2 * x + c, queries, keys, values, out_weight, half, groups)
+    pairs = lax.all_to_all(pairs, "z", 0, 0, tiled=True)
+    weight = lax.all_gather(after(columns, pairs), "z", axis=0, tiled=True)
+    own, behind, ahead, over = two_steps(pairs, "x")
     q = lax.all_to_all(after(grouped, pairs), "z", 0, 0, tiled=True)
-    q_beside = shift(after(q, *moved[1], *moved[2]), "y", 1)
-
-    columns = out_weight.shape[1] // across
-    half = columns // 2
-    mine = lax.dynamic_slice_in_dim(after(out_weight, pairs), x * columns + c * half, half, axis=1)
-    weight = lax.all_gather(mine, "z", axis=0, tiled=True)
-
-    all_pairs = [part for piece in moved for part in (*piece, *(shift(p, "c", 1) for p in piece))]
-    partial_beside = attend(q_beside, all_pairs)
-    partial = attend(after(q, partial_beside), all_pairs)
+    q_beside = shift(after(q, *behind, *ahead), "y", 1)
+
+    every = [part for p in (own, behind, ahead, over) for part in (*p, *(shift(b, "c", 1) for b in p))]
+    partial_beside = attend(q_beside, every)
+    partial = attend(after(q, partial_beside), every)
     attention = merge(partial, shift(partial_beside, "y", 1), groups)
+    weight_beside = shift(after(weight, attention), "c", 1)
 
     back = lax.all_to_all(attention, "z", 0, 0, tiled=True)
-    weight_beside = shift(after(weight, attention), "c", 1)
-    place_c = c.astype(jnp.int32)[None]
-    last = project(place_c, back, weight, weight_beside)
-    returned = [last]
-    there = from_all(back, "x", lambda value: after(value, last))
-    for (piece, *rest), distance in zip(there[1:], (1, -1, 2)):
-        piece = jnp.concatenate([piece, *rest], axis=0) if rest else piece
-        last = project(place_c, after(piece, last), weight, weight_beside)
-        returned.append(shift(last, "x", -distance))
+    own, behind, ahead, over = ring(back, "x")
+    returned, done = [], ()
+    for pieces, distances in (((own,), (0,)), ((behind, ahead), (1, -1)), ((over,), (2,))):
+        pieces = [[after(part, *done) for part in piece] for piece in pieces]
+        done = project(c, pieces, weight, weight_beside)
+        returned += [shift(block, "x", -distance) for block, distance in zip(done, distances)]
     own, ahead, behind, over = returned
-    return place(x.astype(jnp.int32)[None], [own, ahead, over, behind])
+    return place(x, [own, ahead, over, behind])
 
 
 def solution(mesh):

time: 191 us -> 183 us (0.958)
  blocking collectives: 20.1 us -> 55.9 us
  waiting for transfers between devices: 74.5 us -> 42.1 us
  starting transfers between devices: 33 us -> 25 us
    all_to_all x0 -> x1, blocking collectives: none -> 35.8 us  [per_device(): pairs = lax.all_to_all(pairs, 'z', 0, 0, tiled=True)]
    all_to_all x1 -> x0, waiting for transfers between devices: 27.3 us -> none  [per_device(): pairs = lax.all_to_all(grouped_pairs, 'z', 0, 0, tiled=True)]
    all_to_all x1 -> x0, starting transfers between devices: 8.47 us -> none  [per_device(): pairs = lax.all_to_all(grouped_pairs, 'z', 0, 0, tiled=True)]
    ppermute x19 -> x21, waiting for transfers between devices: 47.2 us -> 41.9 us  [shift(): lax.ppermute(block, axis, [(i, (i + distance) % n) for i in range(n)])]
    pallas_call x5 -> x4, Pallas kernels: 13.6 us -> 11.9 us  [the longest x3 8.91 us: project(): pl.pallas_call(functools.partial(project_kernel, pieces=len(pieces)), gri...]
    ppermute x19 -> x21, starting transfers between devices: 21 us -> 21.5 us  [shift(): lax.ppermute(block, axis, [(i, (i + distance) % n) for i in range(n)])]
  transfers between devices with their start and end apart: 22 -> 23, of which waited for: 7 -> 9; matrix products, arithmetic and copies ran while one was open for 1% -> 2% of each run, Pallas kernels for 19% -> 20%
where the time goes in v1:
time: 183 us; the launch traced here: 182 us
  blocking collectives  55.9 us (31%)
  waiting for transfers between devices  42.1 us (23%)
  Pallas kernels  40.9 us (22%)
  starting transfers between devices  25 us (14%)
  between operations  13.5 us (7%)
  local copies, waits for them, and re-layouts  4.88 us (3%)
    ppermute x21, waiting for transfers between devices, shift(): lax.ppermute(block, axis, [(i, (i + distance) % n) for i in range(n)])  41.9 us
    all_to_all x1, blocking collectives, per_device(): pairs = lax.all_to_all(pairs, 'z', 0, 0, tiled=True)  35.8 us
    pallas_call x2, Pallas kernels, attend(): pl.pallas_call(attend_kernel, grid=(heads,), in_specs=[pl.BlockSpec((grou...  27.4 us
    ppermute x21, starting transfers between devices, shift(): lax.ppermute(block, axis, [(i, (i + distance) % n) for i in range(n)])  21.5 us
    all_to_all x1, blocking collectives, per_device(): back = lax.all_to_all(attention, 'z', 0, 0, tiled=True)  20.1 us
    pallas_call x3, Pallas kernels, project(): pl.pallas_call(functools.partial(project_kernel, pieces=len(pieces)), gri...  8.91 us
  transfers between devices with their start and end apart: 23, of which 9 were waited for; matrix products, arithmetic and copies ran while one was open for 2% of the time, Pallas kernels for 20%

profile of v1, /device:TPU:16, one launch (start us, length us, event | category | flops | bytes accessed | tf_op | source)
XLA Modules:
  0.0 182.2 jit_solution(17983877257817853904)
XLA Ops:
  6.5 3.0 %shard_map.46 = (bf16[8,3,80,128]{3,2,1,0:T(8,128)(2,1)}, bf16[8,6,80,128]{3,2,1,0:T(8,128)(2,1)}, bf16[384,640]{1,0:T(8,128)(2,1)}) custom-call(s32[1]{0:T(128)S(6)} %add.3.at_ref, bf16[80,3072]{1,0:T(8,128)(2,1)} %q_ref.1, bf16[80,3072]{1,0:T(8,128)(2,1)} %k_ref.1, bf16[80,3072]{1,0:T(8,128)(2,1)} %v_ref.1, bf16[384,5120]{1,0:T(8,128)(2,1)} %weight_ref.1), custom_call_target="tpu_custom_call" | custom-call | tf_op jit(solution)/shard_map/pallas_call | solution.py:69
  9.5 35.8 %all_to_all.15.refs_0_ = bf16[8,6,80,128]{3,2,1,0:T(8,128)(2,1)S(1)} all-to-all(bf16[8,6,80,128]{3,2,1,0:T(8,128)(2,1)} %get-tuple-element.22), channel_id=1, replica_groups=mesh['clip'=2,'x'=4,'y'=2,'c'=2,'z'=8] {'z'}, dimensions={0} | all-to-all | bytes 1966080 | tf_op jit(solution)/shard_map/all_to_all | solution.py:281
  46.9 1.7 collective-permute-start.1
  48.7 3.5 %all-to-all-start.1 = ((bf16[8,3,80,128]{3,2,1,0:T(8,128)(2,1)}), bf16[8,3,80,128]{3,2,1,0:T(8,128)(2,1)S(1)}, u32[]{:S(2)}, u32[]{:S(2)}) async-start(bf16[8,3,80,128]{3,2,1,0:T(8,128)(2,1)} %get-tuple-element.23), calls=%async_computation.1 | async-start | bytes 983040 | tf_op jit(solution)/shard_map/all_to_all | solution.py:284
  52.1 16.1 %collective-permute-done.refs_2_ = bf16[8,6,80,128]{3,2,1,0:T(8,128)(2,1)S(1)} collective-permute-done((bf16[8,6,80,128]{3,2,1,0:T(8,128)(2,1)S(1)}, bf16[8,6,80,128]{3,2,1,0:T(8,128)(2,1)S(1)}, u32[]{:S(2)}, u32[]{:S(2)}) %collective-permute-start) | collective-permute-done | bytes 983072 | tf_op jit(solution)/shard_map/ppermute | solution.py:22
  69.9 1.8 %slice.17 = bf16[4,6,80,128]{3,2,1,0:T(8,128)(2,1)} slice(bf16[8,6,80,128]{3,2,1,0:T(8,128)(2,1)} %collective-permute-done.1.refs_4_), slice={[4:8], [0:6], [0:80], [0:128]} | slice | bytes 983040 | tf_op jit(solution)/shard_map/slice | solution.py:37
  71.8 3.0 %collective-permute-start.7 = (bf16[4,6,80,128]{3,2,1,0:T(8,128)(2,1)}, bf16[4,6,80,128]{3,2,1,0:T(8,128)(2,1)}, u32[]{:S(2)}, u32[]{:S(2)}) collective-permute-start(bf16[4,6,80,128]{3,2,1,0:T(8,128)(2,1)} %slice.17), channel_id=1, source_target_pairs={{0,96},{32,0},{64,32},{96,64},{1,97},{33,1},{65,33},{97,65},{2,98}... | collective-permute-start | bytes 1474568 | tf_op jit(solution)/shard_map/ppermute | solution.py:22
  76.2 4.8 %collective-permute-done.6.refs_6_ = bf16[4,6,80,128]{3,2,1,0:T(8,128)(2,1)} collective-permute-done((bf16[4,6,80,128]{3,2,1,0:T(8,128)(2,1)}, bf16[4,6,80,128]{3,2,1,0:T(8,128)(2,1)}, u32[]{:S(2)}, u32[]{:S(2)}) %collective-permute-start.6) | collective-permute-done | bytes 491552 | tf_op jit(solution)/shard_map/ppermute | solution.py:22
  81.0 4.8 %collective-permute-done.7.refs_7_ = bf16[4,6,80,128]{3,2,1,0:T(8,128)(2,1)} collective-permute-done((bf16[4,6,80,128]{3,2,1,0:T(8,128)(2,1)}, bf16[4,6,80,128]{3,2,1,0:T(8,128)(2,1)}, u32[]{:S(2)}, u32[]{:S(2)}) %collective-permute-start.7) | collective-permute-done | bytes 491552 | tf_op jit(solution)/shard_map/ppermute | solution.py:22
  85.7 2.4 %collective-permute-done.2.q_ref = bf16[8,3,80,128]{3,2,1,0:T(8,128)(2,1)S(1)} collective-permute-done((bf16[8,3,80,128]{3,2,1,0:T(8,128)(2,1)S(1)}, bf16[8,3,80,128]{3,2,1,0:T(8,128)(2,1)S(1)}, u32[]{:S(2)}, u32[]{:S(2)}) %collective-permute-start.2) | collective-permute-done | bytes 491552 | tf_op jit(solution)/shard_map/ppermute | solution.py:22
  88.1 13.7 %shard_map.47 = bf16[3,672,128]{2,1,0:T(8,128)(2,1)S(1)} custom-call(bf16[8,3,80,128]{3,2,1,0:T(8,128)(2,1)S(1)} %collective-permute-done.2.q_ref, bf16[8,6,80,128]{3,2,1,0:T(8,128)(2,1)S(1)} %all_to_all.15.refs_0_, bf16[8,6,80,128]{3,2,1,0:T(8,128)(2,1)S(1)} %collective-permute-done.3.refs_1_, bf16[8,6,80,128]{3,2,1,0:T(8,128)(2,1)S(1)} %collective-permute-done.refs_2_, ...), custom_call_target="tpu_custom_call" | custom-call | flops 20132659200 | bytes 7864320 | tf_op jit(solution)/shard_map/pallas_call | solution.py:146
  103.4 13.7 %shard_map.48.a_ref = bf16[3,672,128]{2,1,0:T(8,128)(2,1)S(1)} custom-call(bf16[8,3,80,128]{3,2,1,0:T(8,128)(2,1)S(1)} %all-to-all-done.1.q_ref, bf16[8,6,80,128]{3,2,1,0:T(8,128)(2,1)S(1)} %all_to_all.15.refs_0_, bf16[8,6,80,128]{3,2,1,0:T(8,128)(2,1)S(1)} %collective-permute-done.3.refs_1_, bf16[8,6,80,128]{3,2,1,0:T(8,128)(2,1)S(1)} %collective-permute-done.refs_2_, ...), custom_call_target="tpu_custom_call" | custom-call | flops 20132659200 | bytes 7864320 | tf_op jit(solution)/shard_map/pallas_call | solution.py:146
  117.9 20.1 %all_to_all.16.refs_0_.refs_1_ = bf16[8,3,80,128]{3,2,1,0:T(8,128)(2,1)S(1)} all-to-all(bf16[8,3,80,128]{3,2,1,0:T(8,128)(2,1)S(1)} %shard_map.49), channel_id=1, replica_groups=mesh['clip'=2,'x'=4,'y'=2,'c'=2,'z'=8] {'z'}, dimensions={0} | all-to-all | bytes 983040 | tf_op jit(solution)/shard_map/all_to_all | solution.py:293
  139.1 2.7 %collective-permute-start.15 = (bf16[4,3,80,128]{3,2,1,0:T(8,128)(2,1)S(1)}, bf16[4,3,80,128]{3,2,1,0:T(8,128)(2,1)S(1)}, u32[]{:S(2)}, u32[]{:S(2)}) collective-permute-start(bf16[4,3,80,128]{3,2,1,0:T(8,128)(2,1)S(1)} %get-tuple-element.37), channel_id=1, source_target_pairs={{0,96},{32,0},{64,32},{96,64},{1,97},{33,1},{65,33},{97,65},{2,98}... | collective-permute-start | bytes 737288 | tf_op jit(solution)/shard_map/ppermute | solution.py:22
  141.9 1.9 %collective-permute-start.13 = (bf16[4,3,80,128]{3,2,1,0:T(8,128)(2,1)S(1)}, bf16[4,3,80,128]{3,2,1,0:T(8,128)(2,1)S(1)}, u32[]{:S(2)}, u32[]{:S(2)}) collective-permute-start(bf16[4,3,80,128]{3,2,1,0:T(8,128)(2,1)S(1)} %get-tuple-element.38), channel_id=1, source_target_pairs={{0,96},{32,0},{64,32},{96,64},{1,97},{33,1},{65,33},{97,65},{2,98}... | collective-permute-start | bytes 737288 | tf_op jit(solution)/shard_map/ppermute | solution.py:22
  143.9 4.6 %collective-permute-done.12.refs_0_ = bf16[4,3,80,128]{3,2,1,0:T(8,128)(2,1)S(1)} collective-permute-done((bf16[4,3,80,128]{3,2,1,0:T(8,128)(2,1)S(1)}, bf16[4,3,80,128]{3,2,1,0:T(8,128)(2,1)S(1)}, u32[]{:S(2)}, u32[]{:S(2)}) %collective-permute-start.12) | collective-permute-done | bytes 245792 | tf_op jit(solution)/shard_map/ppermute | solution.py:22
  148.6 3.4 %collective-permute-start.18 = (bf16[4,3,80,128]{3,2,1,0:T(8,128)(2,1)S(1)}, bf16[4,3,80,128]{3,2,1,0:T(8,128)(2,1)S(1)}, u32[]{:S(2)}, u32[]{:S(2)}) collective-permute-start(bf16[4,3,80,128]{3,2,1,0:T(8,128)(2,1)S(1)} %collective-permute-done.15.refs_3_), channel_id=1, source_target_pairs={{0,96},{32,0},{64,32},{96,64},{1,97},{33,1},{65,33},{97,65},{2,98}... | collective-permute-start | bytes 737288 | tf_op jit(solution)/shard_map/ppermute | solution.py:22
  151.9 2.1 %copy-done = bf16[3072,640]{1,0:T(8,128)(2,1)S(1)} copy-done((bf16[3072,640]{1,0:T(8,128)(2,1)S(1)}, bf16[3072,640]{1,0:T(8,128)(2,1)}, u32[]{:S(2)}) %copy-start) | copy-done | bytes 3932184
  154.0 2.7 %shard_map.50.refs_0_ = bf16[80,1280]{1,0:T(8,128)(2,1)S(1)} custom-call(s32[1]{0:T(128)} %bitcast.1.c_ref, bf16[8,3,80,128]{3,2,1,0:T(8,128)(2,1)S(1)} %all_to_all.16.refs_0_.refs_1_, bf16[8,3,80,128]{3,2,1,0:T(8,128)(2,1)S(1)} %all_to_all.16.refs_0_.refs_1_, bf16[3072,640]{1,0:T(8,128)(2,1)S(1)} %copy-done, ...), custom_call_target="tpu_custom_call" | custom-call | tf_op jit(solution)/shard_map/pallas_call | solution.py:237
  156.8 3.5 %shard_map.51 = (bf16[80,1280]{1,0:T(8,128)(2,1)S(1)}, bf16[80,1280]{1,0:T(8,128)(2,1)S(1)}) custom-call(s32[1]{0:T(128)} %bitcast.1.c_ref, bf16[4,3,80,128]{3,2,1,0:T(8,128)(2,1)S(1)} %collective-permute-done.12.refs_0_, bf16[4,3,80,128]{3,2,1,0:T(8,128)(2,1)S(1)} %collective-permute-done.13.refs_1_, ...), custom_call_target="tpu_custom_call" | custom-call | tf_op jit(solution)/shard_map/pallas_call | solution.py:237
  161.1 2.7 %shard_map.52 = bf16[80,1280]{1,0:T(8,128)(2,1)S(1)} custom-call(s32[1]{0:T(128)} %bitcast.1.c_ref, bf16[4,3,80,128]{3,2,1,0:T(8,128)(2,1)S(1)} %collective-permute-done.17.refs_0_, bf16[4,3,80,128]{3,2,1,0:T(8,128)(2,1)S(1)} %collective-permute-done.18.refs_1_, bf16[3072,640]{1,0:T(8,128)(2,1)S(1)} %copy-done, ...), custom_call_target="tpu_custom_call" | custom-call | tf_op jit(solution)/shard_map/pallas_call | solution.py:237
  165.3 1.9 %collective-permute-done.16.refs_1_ = bf16[80,1280]{1,0:T(8,128)(2,1)S(1)} collective-permute-done((bf16[80,1280]{1,0:T(8,128)(2,1)S(1)}, bf16[80,1280]{1,0:T(8,128)(2,1)S(1)}, u32[]{:S(2)}, u32[]{:S(2)}) %collective-permute-start.16) | collective-permute-done | bytes 204832 | tf_op jit(solution)/shard_map/ppermute | solution.py:22
  167.2 5.1 %collective-permute-done.19.refs_2_ = bf16[80,1280]{1,0:T(8,128)(2,1)S(1)} collective-permute-done((bf16[80,1280]{1,0:T(8,128)(2,1)S(1)}, bf16[80,1280]{1,0:T(8,128)(2,1)S(1)}, u32[]{:S(2)}, u32[]{:S(2)}) %collective-permute-start.19) | collective-permute-done | bytes 204832 | tf_op jit(solution)/shard_map/ppermute | solution.py:22
  172.3 2.1 %collective-permute-done.20.refs_3_ = bf16[80,1280]{1,0:T(8,128)(2,1)S(1)} collective-permute-done((bf16[80,1280]{1,0:T(8,128)(2,1)S(1)}, bf16[80,1280]{1,0:T(8,128)(2,1)S(1)}, u32[]{:S(2)}, u32[]{:S(2)}) %collective-permute-start.20) | collective-permute-done | bytes 204832 | tf_op jit(solution)/shard_map/ppermute | solution.py:22
  (38 shorter events, 11.5 us)
Async XLA Ops:
  6.5 111.2 %all-gather.2.cloned.1.call-start = ((), (), s32[]{:S(2)}) async-start(), calls=%async_computation.3 | async-start | bytes 4423680 | tf_op jit(solution)/shard_map/all_gather | solution.py:282
  45.3 22.9 %collective-permute-start = (bf16[8,6,80,128]{3,2,1,0:T(8,128)(2,1)S(1)}, bf16[8,6,80,128]{3,2,1,0:T(8,128)(2,1)S(1)}, u32[]{:S(2)}, u32[]{:S(2)}) collective-permute-start(bf16[8,6,80,128]{3,2,1,0:T(8,128)(2,1)S(1)} %all_to_all.15.refs_0_), channel_id=1, source_target_pairs={{0,32},{32,64},{64,96},{96,0},{1,33},{33,65},{65,97},{97,1},{2,34}... | collective-permute-start | bytes 2949128 | tf_op jit(solution)/shard_map/ppermute | solution.py:22
  46.9 22.5 %collective-permute-start.1 = (bf16[8,6,80,128]{3,2,1,0:T(8,128)(2,1)S(1)}, bf16[8,6,80,128]{3,2,1,0:T(8,128)(2,1)}, u32[]{:S(2)}, u32[]{:S(2)}) collective-permute-start(bf16[8,6,80,128]{3,2,1,0:T(8,128)(2,1)S(1)} %all_to_all.15.refs_0_), channel_id=1, source_target_pairs={{0,96},{32,0},{64,32},{96,64},{1,97},{33,1},{65,33},{97,65},{2,98}... | collective-permute-start | bytes 2949128 | tf_op jit(solution)/shard_map/ppermute | solution.py:22
  48.7 26.3 %collective-permute-start.3 = (bf16[8,6,80,128]{3,2,1,0:T(8,128)(2,1)S(1)}, bf16[8,6,80,128]{3,2,1,0:T(8,128)(2,1)S(1)}, u32[]{:S(2)}, u32[]{:S(2)}) collective-permute-start(bf16[8,6,80,128]{3,2,1,0:T(8,128)(2,1)S(1)} %all_to_all.15.refs_0_), channel_id=1, source_target_pairs={{0,8},{8,0},{1,9},{9,1},{2,10},{10,2},{3,11},{11,3},{4,12},{12,4},... | collective-permute-start | bytes 2949128 | tf_op jit(solution)/shard_map/ppermute | solution.py:22
  48.7 26.2 %all-to-all-start.1 = ((bf16[8,3,80,128]{3,2,1,0:T(8,128)(2,1)}), bf16[8,3,80,128]{3,2,1,0:T(8,128)(2,1)S(1)}, u32[]{:S(2)}, u32[]{:S(2)}) async-start(bf16[8,3,80,128]{3,2,1,0:T(8,128)(2,1)} %get-tuple-element.23), calls=%async_computation.1 | async-start | bytes 983040 | tf_op jit(solution)/shard_map/all_to_all | solution.py:284
  69.1 11.8 %collective-permute-start.6 = (bf16[4,6,80,128]{3,2,1,0:T(8,128)(2,1)}, bf16[4,6,80,128]{3,2,1,0:T(8,128)(2,1)}, u32[]{:S(2)}, u32[]{:S(2)}) collective-permute-start(bf16[4,6,80,128]{3,2,1,0:T(8,128)(2,1)} %slice.16), channel_id=1, source_target_pairs={{0,32},{32,64},{64,96},{96,0},{1,33},{33,65},{65,97},{97,1},{2,34}... | collective-permute-start | bytes 1474568 | tf_op jit(solution)/shard_map/ppermute | solution.py:22
  69.4 18.7 %collective-permute-start.4 = (bf16[8,6,80,128]{3,2,1,0:T(8,128)(2,1)S(1)}, bf16[8,6,80,128]{3,2,1,0:T(8,128)(2,1)}, u32[]{:S(2)}, u32[]{:S(2)}) collective-permute-start(bf16[8,6,80,128]{3,2,1,0:T(8,128)(2,1)S(1)} %collective-permute-done.refs_2_), channel_id=1, source_target_pairs={{0,8},{8,0},{1,9},{9,1},{2,10},{10,2},{3,11},{11,3},{4,12},{12,4},... | collective-permute-start | bytes 2949128 | tf_op jit(solution)/shard_map/ppermute | solution.py:22
  69.4 18.7 %collective-permute-start.5 = (bf16[8,6,80,128]{3,2,1,0:T(8,128)(2,1)}, bf16[8,6,80,128]{3,2,1,0:T(8,128)(2,1)}, u32[]{:S(2)}, u32[]{:S(2)}) collective-permute-start(bf16[8,6,80,128]{3,2,1,0:T(8,128)(2,1)} %collective-permute-done.1.refs_4_), channel_id=1, source_target_pairs={{0,8},{8,0},{1,9},{9,1},{2,10},{10,2},{3,11},{11,3},{4,12},{12,4},... | collective-permute-start | bytes 2949128 | tf_op jit(solution)/shard_map/ppermute | solution.py:22
  71.8 13.9 %collective-permute-start.7 = (bf16[4,6,80,128]{3,2,1,0:T(8,128)(2,1)}, bf16[4,6,80,128]{3,2,1,0:T(8,128)(2,1)}, u32[]{:S(2)}, u32[]{:S(2)}) collective-permute-start(bf16[4,6,80,128]{3,2,1,0:T(8,128)(2,1)} %slice.17), channel_id=1, source_target_pairs={{0,96},{32,0},{64,32},{96,64},{1,97},{33,1},{65,33},{97,65},{2,98}... | collective-permute-start | bytes 1474568 | tf_op jit(solution)/shard_map/ppermute | solution.py:22
  74.9 13.2 %collective-permute-start.2 = (bf16[8,3,80,128]{3,2,1,0:T(8,128)(2,1)S(1)}, bf16[8,3,80,128]{3,2,1,0:T(8,128)(2,1)S(1)}, u32[]{:S(2)}, u32[]{:S(2)}) collective-permute-start(bf16[8,3,80,128]{3,2,1,0:T(8,128)(2,1)S(1)} %all-to-all-done.1.q_ref), channel_id=1, source_target_pairs={{0,16},{16,0},{1,17},{17,1},{2,18},{18,2},{3,19},{19,3},{4,20},{20... | collective-permute-start | bytes 1474568 | tf_op jit(solution)/shard_map/ppermute | solution.py:22
  81.0 7.2 %collective-permute-start.8 = (bf16[4,6,80,128]{3,2,1,0:T(8,128)(2,1)}, bf16[4,6,80,128]{3,2,1,0:T(8,128)(2,1)S(1)}, u32[]{:S(2)}, u32[]{:S(2)}) collective-permute-start(bf16[4,6,80,128]{3,2,1,0:T(8,128)(2,1)} %collective-permute-done.6.refs_6_), channel_id=1, source_target_pairs={{0,8},{8,0},{1,9},{9,1},{2,10},{10,2},{3,11},{11,3},{4,12},{12,4},... | collective-permute-start | bytes 1474568 | tf_op jit(solution)/shard_map/ppermute | solution.py:22
  85.7 2.4 %collective-permute-start.9 = (bf16[4,6,80,128]{3,2,1,0:T(8,128)(2,1)}, bf16[4,6,80,128]{3,2,1,0:T(8,128)(2,1)S(1)}, u32[]{:S(2)}, u32[]{:S(2)}) collective-permute-start(bf16[4,6,80,128]{3,2,1,0:T(8,128)(2,1)} %collective-permute-done.7.refs_7_), channel_id=1, source_target_pairs={{0,8},{8,0},{1,9},{9,1},{2,10},{10,2},{3,11},{11,3},{4,12},{12,4},... | collective-permute-start | bytes 1474568 | tf_op jit(solution)/shard_map/ppermute | solution.py:22
  101.8 15.2 %collective-permute-start.10 = (bf16[3,672,128]{2,1,0:T(8,128)(2,1)S(1)}, bf16[3,672,128]{2,1,0:T(8,128)(2,1)S(1)}, u32[]{:S(2)}, u32[]{:S(2)}) collective-permute-start(bf16[3,672,128]{2,1,0:T(8,128)(2,1)S(1)} %shard_map.47), channel_id=1, source_target_pairs={{0,16},{16,0},{1,17},{17,1},{2,18},{18,2},{3,19},{19,3},{4,20},{20... | collective-permute-start | bytes 1548296 | tf_op jit(solution)/shard_map/ppermute | solution.py:22
  117.8 34.1 %collective-permute-start.11 = (bf16[3072,640]{1,0:T(8,128)(2,1)}, bf16[3072,640]{1,0:T(8,128)(2,1)S(1)}, u32[]{:S(2)}, u32[]{:S(2)}) collective-permute-start(bf16[3072,640]{1,0:T(8,128)(2,1)} %all-gather.2.cloned.1.call-done.refs_2_.refs_4_), channel_id=1, source_target_pairs={{0,8},{8,0},{1,9},{9,1},{2,10},{10,2},{3,11},{11,3},{4,12},{12,4},... | collective-permute-start | bytes 11796488 | tf_op jit(solution)/shard_map/ppermute | solution.py:22
  138.0 10.5 %collective-permute-start.12 = (bf16[4,3,80,128]{3,2,1,0:T(8,128)(2,1)S(1)}, bf16[4,3,80,128]{3,2,1,0:T(8,128)(2,1)S(1)}, u32[]{:S(2)}, u32[]{:S(2)}) collective-permute-start(bf16[4,3,80,128]{3,2,1,0:T(8,128)(2,1)S(1)} %get-tuple-element.38), channel_id=1, source_target_pairs={{0,32},{32,64},{64,96},{96,0},{1,33},{33,65},{65,97},{97,1},{2,34}... | collective-permute-start | bytes 737288 | tf_op jit(solution)/shard_map/ppermute | solution.py:22
  139.1 9.4 %collective-permute-start.15 = (bf16[4,3,80,128]{3,2,1,0:T(8,128)(2,1)S(1)}, bf16[4,3,80,128]{3,2,1,0:T(8,128)(2,1)S(1)}, u32[]{:S(2)}, u32[]{:S(2)}) collective-permute-start(bf16[4,3,80,128]{3,2,1,0:T(8,128)(2,1)S(1)} %get-tuple-element.37), channel_id=1, source_target_pairs={{0,96},{32,0},{64,32},{96,64},{1,97},{33,1},{65,33},{97,65},{2,98}... | collective-permute-start | bytes 737288 | tf_op jit(solution)/shard_map/ppermute | solution.py:22
  141.9 14.9 %collective-permute-start.13 = (bf16[4,3,80,128]{3,2,1,0:T(8,128)(2,1)S(1)}, bf16[4,3,80,128]{3,2,1,0:T(8,128)(2,1)S(1)}, u32[]{:S(2)}, u32[]{:S(2)}) collective-permute-start(bf16[4,3,80,128]{3,2,1,0:T(8,128)(2,1)S(1)} %get-tuple-element.38), channel_id=1, source_target_pairs={{0,96},{32,0},{64,32},{96,64},{1,97},{33,1},{65,33},{97,65},{2,98}... | collective-permute-start | bytes 737288 | tf_op jit(solution)/shard_map/ppermute | solution.py:22
  143.8 12.9 %collective-permute-start.14 = (bf16[4,3,80,128]{3,2,1,0:T(8,128)(2,1)S(1)}, bf16[4,3,80,128]{3,2,1,0:T(8,128)(2,1)S(1)}, u32[]{:S(2)}, u32[]{:S(2)}) collective-permute-start(bf16[4,3,80,128]{3,2,1,0:T(8,128)(2,1)S(1)} %get-tuple-element.37), channel_id=1, source_target_pairs={{0,32},{32,64},{64,96},{96,0},{1,33},{33,65},{65,97},{97,1},{2,34}... | collective-permute-start | bytes 737288 | tf_op jit(solution)/shard_map/ppermute | solution.py:22
  148.5 12.6 %collective-permute-start.17 = (bf16[4,3,80,128]{3,2,1,0:T(8,128)(2,1)S(1)}, bf16[4,3,80,128]{3,2,1,0:T(8,128)(2,1)S(1)}, u32[]{:S(2)}, u32[]{:S(2)}) collective-permute-start(bf16[4,3,80,128]{3,2,1,0:T(8,128)(2,1)S(1)} %collective-permute-done.12.refs_0_), channel_id=1, source_target_pairs={{0,32},{32,64},{64,96},{96,0},{1,33},{33,65},{65,97},{97,1},{2,34}... | collective-permute-start | bytes 737288 | tf_op jit(solution)/shard_map/ppermute | solution.py:22
  148.6 12.5 %collective-permute-start.18 = (bf16[4,3,80,128]{3,2,1,0:T(8,128)(2,1)S(1)}, bf16[4,3,80,128]{3,2,1,0:T(8,128)(2,1)S(1)}, u32[]{:S(2)}, u32[]{:S(2)}) collective-permute-start(bf16[4,3,80,128]{3,2,1,0:T(8,128)(2,1)S(1)} %collective-permute-done.15.refs_3_), channel_id=1, source_target_pairs={{0,96},{32,0},{64,32},{96,64},{1,97},{33,1},{65,33},{97,65},{2,98}... | collective-permute-start | bytes 737288 | tf_op jit(solution)/shard_map/ppermute | solution.py:22
  151.9 2.1 %copy-start = (bf16[3072,640]{1,0:T(8,128)(2,1)S(1)}, bf16[3072,640]{1,0:T(8,128)(2,1)}, u32[]{:S(2)}) copy-start(bf16[3072,640]{1,0:T(8,128)(2,1)} %all-gather.2.cloned.1.call-done.refs_2_.refs_4_) | copy-start | bytes 11796484
  160.3 7.0 %collective-permute-start.16 = (bf16[80,1280]{1,0:T(8,128)(2,1)S(1)}, bf16[80,1280]{1,0:T(8,128)(2,1)S(1)}, u32[]{:S(2)}, u32[]{:S(2)}) collective-permute-start(bf16[80,1280]{1,0:T(8,128)(2,1)S(1)} %get-tuple-element.33), channel_id=1, source_target_pairs={{0,96},{32,0},{64,32},{96,64},{1,97},{33,1},{65,33},{97,65},{2,98}... | collective-permute-start | bytes 614408 | tf_op jit(solution)/shard_map/ppermute | solution.py:22
  163.8 8.5 %collective-permute-start.19 = (bf16[80,1280]{1,0:T(8,128)(2,1)S(1)}, bf16[80,1280]{1,0:T(8,128)(2,1)S(1)}, u32[]{:S(2)}, u32[]{:S(2)}) collective-permute-start(bf16[80,1280]{1,0:T(8,128)(2,1)S(1)} %shard_map.52), channel_id=1, source_target_pairs={{0,64},{32,96},{64,0},{96,32},{1,65},{33,97},{65,1},{97,33},{2,66}... | collective-permute-start | bytes 614408 | tf_op jit(solution)/shard_map/ppermute | solution.py:22
  164.2 10.2 %collective-permute-start.20 = (bf16[80,1280]{1,0:T(8,128)(2,1)S(1)}, bf16[80,1280]{1,0:T(8,128)(2,1)S(1)}, u32[]{:S(2)}, u32[]{:S(2)}) collective-permute-start(bf16[80,1280]{1,0:T(8,128)(2,1)S(1)} %get-tuple-element.34), channel_id=1, source_target_pairs={{0,32},{32,64},{64,96},{96,0},{1,33},{33,65},{65,97},{97,1},{2,34}... | collective-permute-start | bytes 614408 | tf_op jit(solution)/shard_map/ppermute | solution.py:22
Sparse Core Ops, SparseCore 0:
  45.5 59.0 all-gather.1

commit v2 on v1

--- a/solution.py
+++ b/solution.py
@@ -228,10 +228,13 @@
     lows, highs = [piece[0] for piece in pieces], [piece[-1] for piece in pieces]
     _, heads, rows, _ = lows[0].shape
     groups = depth // heads // HDIM // steps
-    first = 0 if len(pieces[0]) == 2 else steps // 2
     part = (groups, heads, rows, HDIM)
     low = pl.BlockSpec(part, lambda i, c: (jnp.minimum(i, steps // 2 - 1), 0, 0, 0))
-    high = pl.BlockSpec(part, lambda i, c: (jnp.maximum(i - steps // 2, 0) + first, 0, 0, 0))
+
+    def high(piece):
+        first = 0 if len(piece) == 2 else steps // 2
+        return pl.BlockSpec(part, lambda i, c: (jnp.maximum(i - steps // 2, 0) + first, 0, 0, 0))
+
     weight = pl.BlockSpec((depth // steps, columns), lambda i, c: (i, 0))
     out = jax.ShapeDtypeStruct((rows, 2 * columns), jnp.bfloat16)
     return pl.pallas_call(
@@ -239,7 +242,7 @@
         grid_spec=pltpu.PrefetchScalarGridSpec(
             num_scalar_prefetch=1,
             grid=(steps,),
-            in_specs=[low] * len(pieces) + [high] * len(pieces) + [weight, weight],
+            in_specs=[low] * len(pieces) + [high(piece) for piece in pieces] + [weight, weight],
             out_specs=[pl.BlockSpec(out.shape, lambda i, c: (0, 0))] * len(pieces),
             scratch_shapes=[pltpu.VMEM((len(pieces) * rows, columns), jnp.float32)] * 2,
         ),
@@ -293,7 +296,7 @@
     back = lax.all_to_all(attention, "z", 0, 0, tiled=True)
     own, behind, ahead, over = ring(back, "x")
     returned, done = [], ()
-    for pieces, distances in (((own,), (0,)), ((behind, ahead), (1, -1)), ((over,), (2,))):
+    for pieces, distances in (((own, behind, ahead), (0, 1, -1)), ((over,), (2,))):
         pieces = [[after(part, *done) for part in piece] for piece in pieces]
         done = project(c, pieces, weight, weight_beside)
         returned += [shift(block, "x", -distance) for block, distance in zip(done, distances)]

time: 183 us -> 183 us (level)
  waiting for transfers between devices: 42.1 us -> 46.2 us
  starting transfers between devices: 25 us -> 22.8 us
    ppermute x21, waiting for transfers between devices: 41.9 us -> 46 us  [shift(): lax.ppermute(block, axis, [(i, (i + distance) % n) for i in range(n)])]
    ppermute x21, starting transfers between devices: 21.5 us -> 19.3 us  [shift(): lax.ppermute(block, axis, [(i, (i + distance) % n) for i in range(n)])]
    pallas_call x3 -> x2, Pallas kernels: 8.91 us -> 7.14 us  [project(): pl.pallas_call(functools.partial(project_kernel, pieces=len(pieces)), gri...]
  transfers between devices with their start and end apart: 23 -> 23, of which waited for: 9 -> 10; matrix products, arithmetic and copies ran while one was open for 2% -> 2% of each run, Pallas kernels for 20% -> 18%
where the time goes in v2:
time: 183 us
  blocking collectives  56.1 us (31%)
  waiting for transfers between devices  46.2 us (25%)
  Pallas kernels  39.1 us (21%)
  starting transfers between devices  22.8 us (12%)
  between operations  13.5 us (7%)
  local copies, waits for them, and re-layouts  4.88 us (3%)
    ppermute x21, waiting for transfers between devices, shift(): lax.ppermute(block, axis, [(i, (i + distance) % n) for i in range(n)])  46 us
    all_to_all x1, blocking collectives, per_device(): pairs = lax.all_to_all(pairs, 'z', 0, 0, tiled=True)  35.8 us
    pallas_call x2, Pallas kernels, attend(): pl.pallas_call(attend_kernel, grid=(heads,), in_specs=[pl.BlockSpec((grou...  27.4 us
    all_to_all x1, blocking collectives, per_device(): back = lax.all_to_all(attention, 'z', 0, 0, tiled=True)  20.3 us
    ppermute x21, starting transfers between devices, shift(): lax.ppermute(block, axis, [(i, (i + distance) % n) for i in range(n)])  19.3 us
    pallas_call x2, Pallas kernels, project(): pl.pallas_call(functools.partial(project_kernel, pieces=len(pieces)), gri...  7.14 us
  transfers between devices with their start and end apart: 23, of which 10 were waited for; matrix products, arithmetic and copies ran while one was open for 2% of the time, Pallas kernels for 18%

profile of v2, /device:TPU:16, one launch (start us, length us, event | category | flops | bytes accessed | tf_op | source)
XLA Modules:
  0.0 182.6 jit_solution(878634556666408821)
XLA Ops:
  6.5 3.0 %shard_map.46 = (bf16[8,3,80,128]{3,2,1,0:T(8,128)(2,1)}, bf16[8,6,80,128]{3,2,1,0:T(8,128)(2,1)}, bf16[384,640]{1,0:T(8,128)(2,1)}) custom-call(s32[1]{0:T(128)S(6)} %add.3.at_ref, bf16[80,3072]{1,0:T(8,128)(2,1)} %q_ref.1, bf16[80,3072]{1,0:T(8,128)(2,1)} %k_ref.1, bf16[80,3072]{1,0:T(8,128)(2,1)} %v_ref.1, bf16[384,5120]{1,0:T(8,128)(2,1)} %weight_ref.1), custom_call_target="tpu_custom_call" | custom-call | tf_op jit(solution)/shard_map/pallas_call | solution.py:69
  9.5 35.8 %all_to_all.15.refs_0_ = bf16[8,6,80,128]{3,2,1,0:T(8,128)(2,1)S(1)} all-to-all(bf16[8,6,80,128]{3,2,1,0:T(8,128)(2,1)} %get-tuple-element.19), channel_id=1, replica_groups=mesh['clip'=2,'x'=4,'y'=2,'c'=2,'z'=8] {'z'}, dimensions={0} | all-to-all | bytes 1966080 | tf_op jit(solution)/shard_map/all_to_all | solution.py:284
  45.3 1.6 collective-permute-start
  46.9 1.7 collective-permute-start.1
  48.7 3.5 %all-to-all-start.1 = ((bf16[8,3,80,128]{3,2,1,0:T(8,128)(2,1)}), bf16[8,3,80,128]{3,2,1,0:T(8,128)(2,1)S(1)}, u32[]{:S(2)}, u32[]{:S(2)}) async-start(bf16[8,3,80,128]{3,2,1,0:T(8,128)(2,1)} %get-tuple-element.20), calls=%async_computation.1 | async-start | bytes 983040 | tf_op jit(solution)/shard_map/all_to_all | solution.py:287
  52.1 16.1 %collective-permute-done.refs_2_ = bf16[8,6,80,128]{3,2,1,0:T(8,128)(2,1)S(1)} collective-permute-done((bf16[8,6,80,128]{3,2,1,0:T(8,128)(2,1)S(1)}, bf16[8,6,80,128]{3,2,1,0:T(8,128)(2,1)S(1)}, u32[]{:S(2)}, u32[]{:S(2)}) %collective-permute-start) | collective-permute-done | bytes 983072 | tf_op jit(solution)/shard_map/ppermute | solution.py:22
  69.4 1.9 %slice.17 = bf16[4,6,80,128]{3,2,1,0:T(8,128)(2,1)} slice(bf16[8,6,80,128]{3,2,1,0:T(8,128)(2,1)} %collective-permute-done.1.refs_4_), slice={[4:8], [0:6], [0:80], [0:128]} | slice | bytes 983040 | tf_op jit(solution)/shard_map/slice | solution.py:37
  71.3 3.0 %collective-permute-start.7 = (bf16[4,6,80,128]{3,2,1,0:T(8,128)(2,1)}, bf16[4,6,80,128]{3,2,1,0:T(8,128)(2,1)}, u32[]{:S(2)}, u32[]{:S(2)}) collective-permute-start(bf16[4,6,80,128]{3,2,1,0:T(8,128)(2,1)} %slice.17), channel_id=1, source_target_pairs={{0,96},{32,0},{64,32},{96,64},{1,97},{33,1},{65,33},{97,65},{2,98}... | collective-permute-start | bytes 1474568 | tf_op jit(solution)/shard_map/ppermute | solution.py:22
  76.2 4.8 %collective-permute-done.6.refs_6_ = bf16[4,6,80,128]{3,2,1,0:T(8,128)(2,1)} collective-permute-done((bf16[4,6,80,128]{3,2,1,0:T(8,128)(2,1)}, bf16[4,6,80,128]{3,2,1,0:T(8,128)(2,1)}, u32[]{:S(2)}, u32[]{:S(2)}) %collective-permute-start.6) | collective-permute-done | bytes 491552 | tf_op jit(solution)/shard_map/ppermute | solution.py:22
  82.1 6.0 %collective-permute-done.2.q_ref = bf16[8,3,80,128]{3,2,1,0:T(8,128)(2,1)S(1)} collective-permute-done((bf16[8,3,80,128]{3,2,1,0:T(8,128)(2,1)S(1)}, bf16[8,3,80,128]{3,2,1,0:T(8,128)(2,1)S(1)}, u32[]{:S(2)}, u32[]{:S(2)}) %collective-permute-start.2) | collective-permute-done | bytes 491552 | tf_op jit(solution)/shard_map/ppermute | solution.py:22
  88.1 13.7 %shard_map.47 = bf16[3,672,128]{2,1,0:T(8,128)(2,1)S(1)} custom-call(bf16[8,3,80,128]{3,2,1,0:T(8,128)(2,1)S(1)} %collective-permute-done.2.q_ref, bf16[8,6,80,128]{3,2,1,0:T(8,128)(2,1)S(1)} %all_to_all.15.refs_0_, bf16[8,6,80,128]{3,2,1,0:T(8,128)(2,1)S(1)} %collective-permute-done.3.refs_1_, bf16[8,6,80,128]{3,2,1,0:T(8,128)(2,1)S(1)} %collective-permute-done.refs_2_, ...), custom_call_target="tpu_custom_call" | custom-call | flops 20132659200 | bytes 7864320 | tf_op jit(solution)/shard_map/pallas_call | solution.py:146
  103.4 13.7 %shard_map.48.a_ref = bf16[3,672,128]{2,1,0:T(8,128)(2,1)S(1)} custom-call(bf16[8,3,80,128]{3,2,1,0:T(8,128)(2,1)S(1)} %all-to-all-done.1.q_ref, bf16[8,6,80,128]{3,2,1,0:T(8,128)(2,1)S(1)} %all_to_all.15.refs_0_, bf16[8,6,80,128]{3,2,1,0:T(8,128)(2,1)S(1)} %collective-permute-done.3.refs_1_, bf16[8,6,80,128]{3,2,1,0:T(8,128)(2,1)S(1)} %collective-permute-done.refs_2_, ...), custom_call_target="tpu_custom_call" | custom-call | flops 20132659200 | bytes 7864320 | tf_op jit(solution)/shard_map/pallas_call | solution.py:146
  117.9 20.3 %all_to_all.16.refs_0_.refs_3_ = bf16[8,3,80,128]{3,2,1,0:T(8,128)(2,1)S(1)} all-to-all(bf16[8,3,80,128]{3,2,1,0:T(8,128)(2,1)S(1)} %shard_map.49), channel_id=1, replica_groups=mesh['clip'=2,'x'=4,'y'=2,'c'=2,'z'=8] {'z'}, dimensions={0} | all-to-all | bytes 983040 | tf_op jit(solution)/shard_map/all_to_all | solution.py:296
  140.3 2.5 %collective-permute-start.12 = (bf16[4,3,80,128]{3,2,1,0:T(8,128)(2,1)S(1)}, bf16[4,3,80,128]{3,2,1,0:T(8,128)(2,1)S(1)}, u32[]{:S(2)}, u32[]{:S(2)}) collective-permute-start(bf16[4,3,80,128]{3,2,1,0:T(8,128)(2,1)S(1)} %get-tuple-element.32), channel_id=1, source_target_pairs={{0,96},{32,0},{64,32},{96,64},{1,97},{33,1},{65,33},{97,65},{2,98}... | collective-permute-start | bytes 737288 | tf_op jit(solution)/shard_map/ppermute | solution.py:22
  142.8 4.3 %collective-permute-done.14.refs_5_ = bf16[4,3,80,128]{3,2,1,0:T(8,128)(2,1)S(1)} collective-permute-done((bf16[4,3,80,128]{3,2,1,0:T(8,128)(2,1)S(1)}, bf16[4,3,80,128]{3,2,1,0:T(8,128)(2,1)S(1)}, u32[]{:S(2)}, u32[]{:S(2)}) %collective-permute-start.14) | collective-permute-done | bytes 245792 | tf_op jit(solution)/shard_map/ppermute | solution.py:22
  147.1 2.5 %collective-permute-start.18 = (bf16[4,3,80,128]{3,2,1,0:T(8,128)(2,1)S(1)}, bf16[4,3,80,128]{3,2,1,0:T(8,128)(2,1)S(1)}, u32[]{:S(2)}, u32[]{:S(2)}) collective-permute-start(bf16[4,3,80,128]{3,2,1,0:T(8,128)(2,1)S(1)} %collective-permute-done.14.refs_5_), channel_id=1, source_target_pairs={{0,96},{32,0},{64,32},{96,64},{1,97},{33,1},{65,33},{97,65},{2,98}... | collective-permute-start | bytes 737288 | tf_op jit(solution)/shard_map/ppermute | solution.py:22
  149.6 2.8 %collective-permute-done.12.refs_2_ = bf16[4,3,80,128]{3,2,1,0:T(8,128)(2,1)S(1)} collective-permute-done((bf16[4,3,80,128]{3,2,1,0:T(8,128)(2,1)S(1)}, bf16[4,3,80,128]{3,2,1,0:T(8,128)(2,1)S(1)}, u32[]{:S(2)}, u32[]{:S(2)}) %collective-permute-start.12) | collective-permute-done | bytes 245792 | tf_op jit(solution)/shard_map/ppermute | solution.py:22
  152.4 2.5 %collective-permute-done.13.refs_4_ = bf16[4,3,80,128]{3,2,1,0:T(8,128)(2,1)S(1)} collective-permute-done((bf16[4,3,80,128]{3,2,1,0:T(8,128)(2,1)S(1)}, bf16[4,3,80,128]{3,2,1,0:T(8,128)(2,1)S(1)}, u32[]{:S(2)}, u32[]{:S(2)}) %collective-permute-start.13) | collective-permute-done | bytes 245792 | tf_op jit(solution)/shard_map/ppermute | solution.py:22
  154.9 2.1 %copy-done = bf16[3072,640]{1,0:T(8,128)(2,1)S(1)} copy-done((bf16[3072,640]{1,0:T(8,128)(2,1)S(1)}, bf16[3072,640]{1,0:T(8,128)(2,1)}, u32[]{:S(2)}) %copy-start) | copy-done | bytes 3932184
  157.0 4.4 %shard_map.50 = (bf16[80,1280]{1,0:T(8,128)(2,1)S(1)}, bf16[80,1280]{1,0:T(8,128)(2,1)S(1)}, bf16[80,1280]{1,0:T(8,128)(2,1)S(1)}) custom-call(s32[1]{0:T(128)} %bitcast.1.c_ref, bf16[8,3,80,128]{3,2,1,0:T(8,128)(2,1)S(1)} %all_to_all.16.refs_0_.refs_3_, bf16[4,3,80,128]{3,2,1,0:T(8,128)(2,1)S(1)} %collective-permute-done.11.refs_1_, ...), custom_call_target="tpu_custom_call" | custom-call | tf_op jit(solution)/shard_map/pallas_call | solution.py:240
  161.5 2.7 %shard_map.51 = bf16[80,1280]{1,0:T(8,128)(2,1)S(1)} custom-call(s32[1]{0:T(128)} %bitcast.1.c_ref, bf16[4,3,80,128]{3,2,1,0:T(8,128)(2,1)S(1)} %collective-permute-done.17.refs_0_, bf16[4,3,80,128]{3,2,1,0:T(8,128)(2,1)S(1)} %collective-permute-done.18.refs_1_, bf16[3072,640]{1,0:T(8,128)(2,1)S(1)} %copy-done, ...), custom_call_target="tpu_custom_call" | custom-call | tf_op jit(solution)/shard_map/pallas_call | solution.py:240
  164.3 2.2 %collective-permute-start.16 = (bf16[80,1280]{1,0:T(8,128)(2,1)S(1)}, bf16[80,1280]{1,0:T(8,128)(2,1)S(1)}, u32[]{:S(2)}, u32[]{:S(2)}) collective-permute-start(bf16[80,1280]{1,0:T(8,128)(2,1)S(1)} %get-tuple-element.27), channel_id=1, source_target_pairs={{0,96},{32,0},{64,32},{96,64},{1,97},{33,1},{65,33},{97,65},{2,98}... | collective-permute-start | bytes 614408 | tf_op jit(solution)/shard_map/ppermute | solution.py:22
  166.5 6.2 %collective-permute-done.19.refs_2_ = bf16[80,1280]{1,0:T(8,128)(2,1)S(1)} collective-permute-done((bf16[80,1280]{1,0:T(8,128)(2,1)S(1)}, bf16[80,1280]{1,0:T(8,128)(2,1)S(1)}, u32[]{:S(2)}, u32[]{:S(2)}) %collective-permute-start.19) | collective-permute-done | bytes 204832 | tf_op jit(solution)/shard_map/ppermute | solution.py:22
  172.7 2.1 %collective-permute-done.20.refs_3_ = bf16[80,1280]{1,0:T(8,128)(2,1)S(1)} collective-permute-done((bf16[80,1280]{1,0:T(8,128)(2,1)S(1)}, bf16[80,1280]{1,0:T(8,128)(2,1)S(1)}, u32[]{:S(2)}, u32[]{:S(2)}) %collective-permute-start.20) | collective-permute-done | bytes 204832 | tf_op jit(solution)/shard_map/ppermute | solution.py:22
  (37 shorter events, 9.8 us)
Async XLA Ops:
  6.5 111.2 %all-gather.2.cloned.1.call-start = ((), (), s32[]{:S(2)}) async-start(), calls=%async_computation.3 | async-start | bytes 4423680 | tf_op jit(solution)/shard_map/all_gather | solution.py:285
  45.3 22.9 %collective-permute-start = (bf16[8,6,80,128]{3,2,1,0:T(8,128)(2,1)S(1)}, bf16[8,6,80,128]{3,2,1,0:T(8,128)(2,1)S(1)}, u32[]{:S(2)}, u32[]{:S(2)}) collective-permute-start(bf16[8,6,80,128]{3,2,1,0:T(8,128)(2,1)S(1)} %all_to_all.15.refs_0_), channel_id=1, source_target_pairs={{0,32},{32,64},{64,96},{96,0},{1,33},{33,65},{65,97},{97,1},{2,34}... | collective-permute-start | bytes 2949128 | tf_op jit(solution)/shard_map/ppermute | solution.py:22
  46.9 22.5 %collective-permute-start.1 = (bf16[8,6,80,128]{3,2,1,0:T(8,128)(2,1)S(1)}, bf16[8,6,80,128]{3,2,1,0:T(8,128)(2,1)}, u32[]{:S(2)}, u32[]{:S(2)}) collective-permute-start(bf16[8,6,80,128]{3,2,1,0:T(8,128)(2,1)S(1)} %all_to_all.15.refs_0_), channel_id=1, source_target_pairs={{0,96},{32,0},{64,32},{96,64},{1,97},{33,1},{65,33},{97,65},{2,98}... | collective-permute-start | bytes 2949128 | tf_op jit(solution)/shard_map/ppermute | solution.py:22
  48.7 26.3 %collective-permute-start.3 = (bf16[8,6,80,128]{3,2,1,0:T(8,128)(2,1)S(1)}, bf16[8,6,80,128]{3,2,1,0:T(8,128)(2,1)S(1)}, u32[]{:S(2)}, u32[]{:S(2)}) collective-permute-start(bf16[8,6,80,128]{3,2,1,0:T(8,128)(2,1)S(1)} %all_to_all.15.refs_0_), channel_id=1, source_target_pairs={{0,8},{8,0},{1,9},{9,1},{2,10},{10,2},{3,11},{11,3},{4,12},{12,4},... | collective-permute-start | bytes 2949128 | tf_op jit(solution)/shard_map/ppermute | solution.py:22
  48.7 26.2 %all-to-all-start.1 = ((bf16[8,3,80,128]{3,2,1,0:T(8,128)(2,1)}), bf16[8,3,80,128]{3,2,1,0:T(8,128)(2,1)S(1)}, u32[]{:S(2)}, u32[]{:S(2)}) async-start(bf16[8,3,80,128]{3,2,1,0:T(8,128)(2,1)} %get-tuple-element.20), calls=%async_computation.1 | async-start | bytes 983040 | tf_op jit(solution)/shard_map/all_to_all | solution.py:287
  69.1 11.8 %collective-permute-start.6 = (bf16[4,6,80,128]{3,2,1,0:T(8,128)(2,1)}, bf16[4,6,80,128]{3,2,1,0:T(8,128)(2,1)}, u32[]{:S(2)}, u32[]{:S(2)}) collective-permute-start(bf16[4,6,80,128]{3,2,1,0:T(8,128)(2,1)} %slice.16), channel_id=1, source_target_pairs={{0,32},{32,64},{64,96},{96,0},{1,33},{33,65},{65,97},{97,1},{2,34}... | collective-permute-start | bytes 1474568 | tf_op jit(solution)/shard_map/ppermute | solution.py:22
  71.3 10.8 %collective-permute-start.7 = (bf16[4,6,80,128]{3,2,1,0:T(8,128)(2,1)}, bf16[4,6,80,128]{3,2,1,0:T(8,128)(2,1)}, u32[]{:S(2)}, u32[]{:S(2)}) collective-permute-start(bf16[4,6,80,128]{3,2,1,0:T(8,128)(2,1)} %slice.17), channel_id=1, source_target_pairs={{0,96},{32,0},{64,32},{96,64},{1,97},{33,1},{65,33},{97,65},{2,98}... | collective-permute-start | bytes 1474568 | tf_op jit(solution)/shard_map/ppermute | solution.py:22
  74.2 13.9 %collective-permute-start.4 = (bf16[8,6,80,128]{3,2,1,0:T(8,128)(2,1)S(1)}, bf16[8,6,80,128]{3,2,1,0:T(8,128)(2,1)}, u32[]{:S(2)}, u32[]{:S(2)}) collective-permute-start(bf16[8,6,80,128]{3,2,1,0:T(8,128)(2,1)S(1)} %collective-permute-done.refs_2_), channel_id=1, source_target_pairs={{0,8},{8,0},{1,9},{9,1},{2,10},{10,2},{3,11},{11,3},{4,12},{12,4},... | collective-permute-start | bytes 2949128 | tf_op jit(solution)/shard_map/ppermute | solution.py:22
  74.2 13.9 %collective-permute-start.5 = (bf16[8,6,80,128]{3,2,1,0:T(8,128)(2,1)}, bf16[8,6,80,128]{3,2,1,0:T(8,128)(2,1)}, u32[]{:S(2)}, u32[]{:S(2)}) collective-permute-start(bf16[8,6,80,128]{3,2,1,0:T(8,128)(2,1)} %collective-permute-done.1.refs_4_), channel_id=1, source_target_pairs={{0,8},{8,0},{1,9},{9,1},{2,10},{10,2},{3,11},{11,3},{4,12},{12,4},... | collective-permute-start | bytes 2949128 | tf_op jit(solution)/shard_map/ppermute | solution.py:22
  74.9 13.2 %collective-permute-start.2 = (bf16[8,3,80,128]{3,2,1,0:T(8,128)(2,1)S(1)}, bf16[8,3,80,128]{3,2,1,0:T(8,128)(2,1)S(1)}, u32[]{:S(2)}, u32[]{:S(2)}) collective-permute-start(bf16[8,3,80,128]{3,2,1,0:T(8,128)(2,1)S(1)} %all-to-all-done.1.q_ref), channel_id=1, source_target_pairs={{0,16},{16,0},{1,17},{17,1},{2,18},{18,2},{3,19},{19,3},{4,20},{20... | collective-permute-start | bytes 1474568 | tf_op jit(solution)/shard_map/ppermute | solution.py:22
  81.0 7.1 %collective-permute-start.8 = (bf16[4,6,80,128]{3,2,1,0:T(8,128)(2,1)}, bf16[4,6,80,128]{3,2,1,0:T(8,128)(2,1)S(1)}, u32[]{:S(2)}, u32[]{:S(2)}) collective-permute-start(bf16[4,6,80,128]{3,2,1,0:T(8,128)(2,1)} %collective-permute-done.6.refs_6_), channel_id=1, source_target_pairs={{0,8},{8,0},{1,9},{9,1},{2,10},{10,2},{3,11},{11,3},{4,12},{12,4},... | collective-permute-start | bytes 1474568 | tf_op jit(solution)/shard_map/ppermute | solution.py:22
  82.1 6.0 %collective-permute-start.9 = (bf16[4,6,80,128]{3,2,1,0:T(8,128)(2,1)}, bf16[4,6,80,128]{3,2,1,0:T(8,128)(2,1)S(1)}, u32[]{:S(2)}, u32[]{:S(2)}) collective-permute-start(bf16[4,6,80,128]{3,2,1,0:T(8,128)(2,1)} %collective-permute-done.7.refs_7_), channel_id=1, source_target_pairs={{0,8},{8,0},{1,9},{9,1},{2,10},{10,2},{3,11},{11,3},{4,12},{12,4},... | collective-permute-start | bytes 1474568 | tf_op jit(solution)/shard_map/ppermute | solution.py:22
  101.8 15.2 %collective-permute-start.10 = (bf16[3,672,128]{2,1,0:T(8,128)(2,1)S(1)}, bf16[3,672,128]{2,1,0:T(8,128)(2,1)S(1)}, u32[]{:S(2)}, u32[]{:S(2)}) collective-permute-start(bf16[3,672,128]{2,1,0:T(8,128)(2,1)S(1)} %shard_map.47), channel_id=1, source_target_pairs={{0,16},{16,0},{1,17},{17,1},{2,18},{18,2},{3,19},{19,3},{4,20},{20... | collective-permute-start | bytes 1548296 | tf_op jit(solution)/shard_map/ppermute | solution.py:22
  117.8 37.1 %collective-permute-start.15 = (bf16[3072,640]{1,0:T(8,128)(2,1)}, bf16[3072,640]{1,0:T(8,128)(2,1)S(1)}, u32[]{:S(2)}, u32[]{:S(2)}) collective-permute-start(bf16[3072,640]{1,0:T(8,128)(2,1)} %all-gather.2.cloned.1.call-done.refs_6_.refs_2_), channel_id=1, source_target_pairs={{0,8},{8,0},{1,9},{9,1},{2,10},{10,2},{3,11},{11,3},{4,12},{12,4},... | collective-permute-start | bytes 11796488 | tf_op jit(solution)/shard_map/ppermute | solution.py:22
  138.2 8.9 %collective-permute-start.14 = (bf16[4,3,80,128]{3,2,1,0:T(8,128)(2,1)S(1)}, bf16[4,3,80,128]{3,2,1,0:T(8,128)(2,1)S(1)}, u32[]{:S(2)}, u32[]{:S(2)}) collective-permute-start(bf16[4,3,80,128]{3,2,1,0:T(8,128)(2,1)S(1)} %get-tuple-element.31), channel_id=1, source_target_pairs={{0,96},{32,0},{64,32},{96,64},{1,97},{33,1},{65,33},{97,65},{2,98}... | collective-permute-start | bytes 737288 | tf_op jit(solution)/shard_map/ppermute | solution.py:22
  139.6 10.1 %collective-permute-start.11 = (bf16[4,3,80,128]{3,2,1,0:T(8,128)(2,1)S(1)}, bf16[4,3,80,128]{3,2,1,0:T(8,128)(2,1)S(1)}, u32[]{:S(2)}, u32[]{:S(2)}) collective-permute-start(bf16[4,3,80,128]{3,2,1,0:T(8,128)(2,1)S(1)} %get-tuple-element.32), channel_id=1, source_target_pairs={{0,32},{32,64},{64,96},{96,0},{1,33},{33,65},{65,97},{97,1},{2,34}... | collective-permute-start | bytes 737288 | tf_op jit(solution)/shard_map/ppermute | solution.py:22
  140.3 12.1 %collective-permute-start.12 = (bf16[4,3,80,128]{3,2,1,0:T(8,128)(2,1)S(1)}, bf16[4,3,80,128]{3,2,1,0:T(8,128)(2,1)S(1)}, u32[]{:S(2)}, u32[]{:S(2)}) collective-permute-start(bf16[4,3,80,128]{3,2,1,0:T(8,128)(2,1)S(1)} %get-tuple-element.32), channel_id=1, source_target_pairs={{0,96},{32,0},{64,32},{96,64},{1,97},{33,1},{65,33},{97,65},{2,98}... | collective-permute-start | bytes 737288 | tf_op jit(solution)/shard_map/ppermute | solution.py:22
  142.8 12.1 %collective-permute-start.13 = (bf16[4,3,80,128]{3,2,1,0:T(8,128)(2,1)S(1)}, bf16[4,3,80,128]{3,2,1,0:T(8,128)(2,1)S(1)}, u32[]{:S(2)}, u32[]{:S(2)}) collective-permute-start(bf16[4,3,80,128]{3,2,1,0:T(8,128)(2,1)S(1)} %get-tuple-element.31), channel_id=1, source_target_pairs={{0,32},{32,64},{64,96},{96,0},{1,33},{33,65},{65,97},{97,1},{2,34}... | collective-permute-start | bytes 737288 | tf_op jit(solution)/shard_map/ppermute | solution.py:22
  147.1 14.3 %collective-permute-start.18 = (bf16[4,3,80,128]{3,2,1,0:T(8,128)(2,1)S(1)}, bf16[4,3,80,128]{3,2,1,0:T(8,128)(2,1)S(1)}, u32[]{:S(2)}, u32[]{:S(2)}) collective-permute-start(bf16[4,3,80,128]{3,2,1,0:T(8,128)(2,1)S(1)} %collective-permute-done.14.refs_5_), channel_id=1, source_target_pairs={{0,96},{32,0},{64,32},{96,64},{1,97},{33,1},{65,33},{97,65},{2,98}... | collective-permute-start | bytes 737288 | tf_op jit(solution)/shard_map/ppermute | solution.py:22
  149.6 11.8 %collective-permute-start.17 = (bf16[4,3,80,128]{3,2,1,0:T(8,128)(2,1)S(1)}, bf16[4,3,80,128]{3,2,1,0:T(8,128)(2,1)S(1)}, u32[]{:S(2)}, u32[]{:S(2)}) collective-permute-start(bf16[4,3,80,128]{3,2,1,0:T(8,128)(2,1)S(1)} %collective-permute-done.11.refs_1_), channel_id=1, source_target_pairs={{0,32},{32,64},{64,96},{96,0},{1,33},{33,65},{65,97},{97,1},{2,34}... | collective-permute-start | bytes 737288 | tf_op jit(solution)/shard_map/ppermute | solution.py:22
  154.9 2.1 %copy-start = (bf16[3072,640]{1,0:T(8,128)(2,1)S(1)}, bf16[3072,640]{1,0:T(8,128)(2,1)}, u32[]{:S(2)}) copy-start(bf16[3072,640]{1,0:T(8,128)(2,1)} %all-gather.2.cloned.1.call-done.refs_6_.refs_2_) | copy-start | bytes 11796484
  164.2 8.5 %collective-permute-start.19 = (bf16[80,1280]{1,0:T(8,128)(2,1)S(1)}, bf16[80,1280]{1,0:T(8,128)(2,1)S(1)}, u32[]{:S(2)}, u32[]{:S(2)}) collective-permute-start(bf16[80,1280]{1,0:T(8,128)(2,1)S(1)} %shard_map.51), channel_id=1, source_target_pairs={{0,64},{32,96},{64,0},{96,32},{1,65},{33,97},{65,1},{97,33},{2,66}... | collective-permute-start | bytes 614408 | tf_op jit(solution)/shard_map/ppermute | solution.py:22
  164.3 8.4 %collective-permute-start.16 = (bf16[80,1280]{1,0:T(8,128)(2,1)S(1)}, bf16[80,1280]{1,0:T(8,128)(2,1)S(1)}, u32[]{:S(2)}, u32[]{:S(2)}) collective-permute-start(bf16[80,1280]{1,0:T(8,128)(2,1)S(1)} %get-tuple-element.27), channel_id=1, source_target_pairs={{0,96},{32,0},{64,32},{96,64},{1,97},{33,1},{65,33},{97,65},{2,98}... | collective-permute-start | bytes 614408 | tf_op jit(solution)/shard_map/ppermute | solution.py:22
  166.5 8.3 %collective-permute-start.20 = (bf16[80,1280]{1,0:T(8,128)(2,1)S(1)}, bf16[80,1280]{1,0:T(8,128)(2,1)S(1)}, u32[]{:S(2)}, u32[]{:S(2)}) collective-permute-start(bf16[80,1280]{1,0:T(8,128)(2,1)S(1)} %get-tuple-element.28), channel_id=1, source_target_pairs={{0,32},{32,64},{64,96},{96,0},{1,33},{33,65},{65,97},{97,1},{2,34}... | collective-permute-start | bytes 614408 | tf_op jit(solution)/shard_map/ppermute | solution.py:22
Sparse Core Ops, SparseCore 0:
  45.5 59.0 all-gather.1

commit v3 on v2

--- a/solution.py
+++ b/solution.py
@@ -247,7 +247,7 @@
             scratch_shapes=[pltpu.VMEM((len(pieces) * rows, columns), jnp.float32)] * 2,
         ),
         out_shape=[out] * len(pieces),
-        compiler_params=params(16),
+        compiler_params=params(56),
     )(c, *lows, *highs, near, far)
 
 

time: 183 us -> 192 us (1.049)
  Pallas kernels: 39.1 us -> 45.8 us
    pallas_call x2, Pallas kernels: 7.14 us -> 13.8 us  [project(): pl.pallas_call(functools.partial(project_kernel, pieces=len(pieces)), gri...]
    unnamed x2 -> x22, local copies, waits for them, and re-layouts: 2.11 us -> 3.97 us
  transfers between devices with their start and end apart: 23 -> 23, of which waited for: 10 -> 11; matrix products, arithmetic and copies ran while one was open for 2% -> 1% of each run, Pallas kernels for 18% -> 19%
where the time goes in v3:
time: 192 us; the launch traced here: 191 us
  blocking collectives  56.1 us (29%)
  waiting for transfers between devices  46.4 us (24%)
  Pallas kernels  45.8 us (24%)
  starting transfers between devices  22.7 us (12%)
  between operations  13.6 us (7%)
  local copies, waits for them, and re-layouts  6.71 us (3%)
    ppermute x21, waiting for transfers between devices, shift(): lax.ppermute(block, axis, [(i, (i + distance) % n) for i in range(n)])  46.2 us
    all_to_all x1, blocking collectives, per_device(): pairs = lax.all_to_all(pairs, 'z', 0, 0, tiled=True)  35.8 us
    pallas_call x2, Pallas kernels, attend(): pl.pallas_call(attend_kernel, grid=(heads,), in_specs=[pl.BlockSpec((grou...  27.4 us
    all_to_all x1, blocking collectives, per_device(): back = lax.all_to_all(attention, 'z', 0, 0, tiled=True)  20.3 us
    ppermute x21, starting transfers between devices, shift(): lax.ppermute(block, axis, [(i, (i + distance) % n) for i in range(n)])  19.2 us
    pallas_call x2, Pallas kernels, project(): pl.pallas_call(functools.partial(project_kernel, pieces=len(pieces)), gri...  13.8 us
    unnamed x22, local copies, waits for them, and re-layouts  3.97 us
  transfers between devices with their start and end apart: 23, of which 11 were waited for; matrix products, arithmetic and copies ran while one was open for 1% of the time, Pallas kernels for 19%

profile of v3, /device:TPU:16, one launch (start us, length us, event | category | flops | bytes accessed | tf_op | source)
XLA Modules:
  0.0 191.2 jit_solution(15944404666503301649)
XLA Ops:
  6.5 3.0 %shard_map.46 = (bf16[8,3,80,128]{3,2,1,0:T(8,128)(2,1)}, bf16[8,6,80,128]{3,2,1,0:T(8,128)(2,1)}, bf16[384,640]{1,0:T(8,128)(2,1)}) custom-call(s32[1]{0:T(128)S(6)} %add.3.at_ref, bf16[80,3072]{1,0:T(8,128)(2,1)} %q_ref.1, bf16[80,3072]{1,0:T(8,128)(2,1)} %k_ref.1, bf16[80,3072]{1,0:T(8,128)(2,1)} %v_ref.1, bf16[384,5120]{1,0:T(8,128)(2,1)} %weight_ref.1), custom_call_target="tpu_custom_call" | custom-call | tf_op jit(solution)/shard_map/pallas_call | solution.py:69
  9.5 35.8 %all_to_all.15.refs_0_ = bf16[8,6,80,128]{3,2,1,0:T(8,128)(2,1)S(1)} all-to-all(bf16[8,6,80,128]{3,2,1,0:T(8,128)(2,1)} %get-tuple-element.19), channel_id=1, replica_groups=mesh['clip'=2,'x'=4,'y'=2,'c'=2,'z'=8] {'z'}, dimensions={0} | all-to-all | bytes 1966080 | tf_op jit(solution)/shard_map/all_to_all | solution.py:284
  45.3 1.6 collective-permute-start
  46.9 1.7 collective-permute-start.1
  48.7 3.5 %all-to-all-start.1 = ((bf16[8,3,80,128]{3,2,1,0:T(8,128)(2,1)}), bf16[8,3,80,128]{3,2,1,0:T(8,128)(2,1)S(1)}, u32[]{:S(2)}, u32[]{:S(2)}) async-start(bf16[8,3,80,128]{3,2,1,0:T(8,128)(2,1)} %get-tuple-element.20), calls=%async_computation.1 | async-start | bytes 983040 | tf_op jit(solution)/shard_map/all_to_all | solution.py:287
  52.2 16.1 %collective-permute-done.refs_2_ = bf16[8,6,80,128]{3,2,1,0:T(8,128)(2,1)S(1)} collective-permute-done((bf16[8,6,80,128]{3,2,1,0:T(8,128)(2,1)S(1)}, bf16[8,6,80,128]{3,2,1,0:T(8,128)(2,1)S(1)}, u32[]{:S(2)}, u32[]{:S(2)}) %collective-permute-start) | collective-permute-done | bytes 983072 | tf_op jit(solution)/shard_map/ppermute | solution.py:22
  69.4 1.8 slice.17
  71.3 3.0 %collective-permute-start.7 = (bf16[4,6,80,128]{3,2,1,0:T(8,128)(2,1)}, bf16[4,6,80,128]{3,2,1,0:T(8,128)(2,1)}, u32[]{:S(2)}, u32[]{:S(2)}) collective-permute-start(bf16[4,6,80,128]{3,2,1,0:T(8,128)(2,1)} %slice.17), channel_id=1, source_target_pairs={{0,96},{32,0},{64,32},{96,64},{1,97},{33,1},{65,33},{97,65},{2,98}... | collective-permute-start | bytes 1474568 | tf_op jit(solution)/shard_map/ppermute | solution.py:22
  76.2 4.8 %collective-permute-done.6.refs_6_ = bf16[4,6,80,128]{3,2,1,0:T(8,128)(2,1)} collective-permute-done((bf16[4,6,80,128]{3,2,1,0:T(8,128)(2,1)}, bf16[4,6,80,128]{3,2,1,0:T(8,128)(2,1)}, u32[]{:S(2)}, u32[]{:S(2)}) %collective-permute-start.6) | collective-permute-done | bytes 491552 | tf_op jit(solution)/shard_map/ppermute | solution.py:22
  82.1 6.0 %collective-permute-done.2.q_ref = bf16[8,3,80,128]{3,2,1,0:T(8,128)(2,1)S(1)} collective-permute-done((bf16[8,3,80,128]{3,2,1,0:T(8,128)(2,1)S(1)}, bf16[8,3,80,128]{3,2,1,0:T(8,128)(2,1)S(1)}, u32[]{:S(2)}, u32[]{:S(2)}) %collective-permute-start.2) | collective-permute-done | bytes 491552 | tf_op jit(solution)/shard_map/ppermute | solution.py:22
  88.1 13.7 %shard_map.47 = bf16[3,672,128]{2,1,0:T(8,128)(2,1)S(1)} custom-call(bf16[8,3,80,128]{3,2,1,0:T(8,128)(2,1)S(1)} %collective-permute-done.2.q_ref, bf16[8,6,80,128]{3,2,1,0:T(8,128)(2,1)S(1)} %all_to_all.15.refs_0_, bf16[8,6,80,128]{3,2,1,0:T(8,128)(2,1)S(1)} %collective-permute-done.3.refs_1_, bf16[8,6,80,128]{3,2,1,0:T(8,128)(2,1)S(1)} %collective-permute-done.refs_2_, ...), custom_call_target="tpu_custom_call" | custom-call | flops 20132659200 | bytes 7864320 | tf_op jit(solution)/shard_map/pallas_call | solution.py:146
  103.4 13.7 %shard_map.48.a_ref = bf16[3,672,128]{2,1,0:T(8,128)(2,1)S(1)} custom-call(bf16[8,3,80,128]{3,2,1,0:T(8,128)(2,1)S(1)} %all-to-all-done.1.q_ref, bf16[8,6,80,128]{3,2,1,0:T(8,128)(2,1)S(1)} %all_to_all.15.refs_0_, bf16[8,6,80,128]{3,2,1,0:T(8,128)(2,1)S(1)} %collective-permute-done.3.refs_1_, bf16[8,6,80,128]{3,2,1,0:T(8,128)(2,1)S(1)} %collective-permute-done.refs_2_, ...), custom_call_target="tpu_custom_call" | custom-call | flops 20132659200 | bytes 7864320 | tf_op jit(solution)/shard_map/pallas_call | solution.py:146
  117.9 20.3 %all_to_all.16.refs_0_.refs_3_ = bf16[8,3,80,128]{3,2,1,0:T(8,128)(2,1)S(1)} all-to-all(bf16[8,3,80,128]{3,2,1,0:T(8,128)(2,1)S(1)} %shard_map.49), channel_id=1, replica_groups=mesh['clip'=2,'x'=4,'y'=2,'c'=2,'z'=8] {'z'}, dimensions={0} | all-to-all | bytes 983040 | tf_op jit(solution)/shard_map/all_to_all | solution.py:296
  140.3 2.4 %collective-permute-start.12 = (bf16[4,3,80,128]{3,2,1,0:T(8,128)(2,1)S(1)}, bf16[4,3,80,128]{3,2,1,0:T(8,128)(2,1)S(1)}, u32[]{:S(2)}, u32[]{:S(2)}) collective-permute-start(bf16[4,3,80,128]{3,2,1,0:T(8,128)(2,1)S(1)} %get-tuple-element.32), channel_id=1, source_target_pairs={{0,96},{32,0},{64,32},{96,64},{1,97},{33,1},{65,33},{97,65},{2,98}... | collective-permute-start | bytes 737288 | tf_op jit(solution)/shard_map/ppermute | solution.py:22
  142.8 4.3 %collective-permute-done.14.refs_5_ = bf16[4,3,80,128]{3,2,1,0:T(8,128)(2,1)S(1)} collective-permute-done((bf16[4,3,80,128]{3,2,1,0:T(8,128)(2,1)S(1)}, bf16[4,3,80,128]{3,2,1,0:T(8,128)(2,1)S(1)}, u32[]{:S(2)}, u32[]{:S(2)}) %collective-permute-start.14) | collective-permute-done | bytes 245792 | tf_op jit(solution)/shard_map/ppermute | solution.py:22
  147.1 2.4 %collective-permute-start.18 = (bf16[4,3,80,128]{3,2,1,0:T(8,128)(2,1)S(1)}, bf16[4,3,80,128]{3,2,1,0:T(8,128)(2,1)S(1)}, u32[]{:S(2)}, u32[]{:S(2)}) collective-permute-start(bf16[4,3,80,128]{3,2,1,0:T(8,128)(2,1)S(1)} %collective-permute-done.14.refs_5_), channel_id=1, source_target_pairs={{0,96},{32,0},{64,32},{96,64},{1,97},{33,1},{65,33},{97,65},{2,98}... | collective-permute-start | bytes 737288 | tf_op jit(solution)/shard_map/ppermute | solution.py:22
  149.6 2.8 %collective-permute-done.12.refs_2_ = bf16[4,3,80,128]{3,2,1,0:T(8,128)(2,1)S(1)} collective-permute-done((bf16[4,3,80,128]{3,2,1,0:T(8,128)(2,1)S(1)}, bf16[4,3,80,128]{3,2,1,0:T(8,128)(2,1)S(1)}, u32[]{:S(2)}, u32[]{:S(2)}) %collective-permute-start.12) | collective-permute-done | bytes 245792 | tf_op jit(solution)/shard_map/ppermute | solution.py:22
  152.4 2.5 %collective-permute-done.13.refs_4_ = bf16[4,3,80,128]{3,2,1,0:T(8,128)(2,1)S(1)} collective-permute-done((bf16[4,3,80,128]{3,2,1,0:T(8,128)(2,1)S(1)}, bf16[4,3,80,128]{3,2,1,0:T(8,128)(2,1)S(1)}, u32[]{:S(2)}, u32[]{:S(2)}) %collective-permute-start.13) | collective-permute-done | bytes 245792 | tf_op jit(solution)/shard_map/ppermute | solution.py:22
  155.6 1.9 copy-done.1
  157.5 7.7 %shard_map.50 = (bf16[80,1280]{1,0:T(8,128)(2,1)}, bf16[80,1280]{1,0:T(8,128)(2,1)}, bf16[80,1280]{1,0:T(8,128)(2,1)}) custom-call(s32[1]{0:T(128)} %bitcast.1.c_ref, bf16[8,3,80,128]{3,2,1,0:T(8,128)(2,1)} %copy-done.2, bf16[4,3,80,128]{3,2,1,0:T(8,128)(2,1)} %copy-done.4, bf16[4,3,80,128]{3,2,1,0:T(8,128)(2,1)} %copy-done.6, ...), custom_call_target="tpu_custom_call" | custom-call | tf_op jit(solution)/shard_map/pallas_call | solution.py:240
  166.6 6.1 %shard_map.51 = bf16[80,1280]{1,0:T(8,128)(2,1)} custom-call(s32[1]{0:T(128)} %bitcast.1.c_ref, bf16[4,3,80,128]{3,2,1,0:T(8,128)(2,1)} %copy-done.7, bf16[4,3,80,128]{3,2,1,0:T(8,128)(2,1)} %copy-done.5, bf16[3072,640]{1,0:T(8,128)(2,1)} %all-gather.2.cloned.1.call-done.refs_6_.refs_2_, bf16[3072,640]{1,0:T(8,128)(2,1)} %copy-done.1), custom_call_target="tpu_custom_call" | custom-call | tf_op jit(solution)/shard_map/pallas_call | solution.py:240
  172.7 2.3 %collective-permute-start.16 = (bf16[80,1280]{1,0:T(8,128)(2,1)S(1)}, bf16[80,1280]{1,0:T(8,128)(2,1)S(1)}, u32[]{:S(2)}, u32[]{:S(2)}) collective-permute-start(bf16[80,1280]{1,0:T(8,128)(2,1)S(1)} %copy-done.10), channel_id=1, source_target_pairs={{0,96},{32,0},{64,32},{96,64},{1,97},{33,1},{65,33},{97,65},{2,98}... | collective-permute-start | bytes 614408 | tf_op jit(solution)/shard_map/ppermute | solution.py:22
  175.0 6.4 %collective-permute-done.19.refs_2_ = bf16[80,1280]{1,0:T(8,128)(2,1)S(1)} collective-permute-done((bf16[80,1280]{1,0:T(8,128)(2,1)}, bf16[80,1280]{1,0:T(8,128)(2,1)S(1)}, u32[]{:S(2)}, u32[]{:S(2)}) %collective-permute-start.19) | collective-permute-done | bytes 204832 | tf_op jit(solution)/shard_map/ppermute | solution.py:22
  181.5 2.0 %collective-permute-done.20.refs_3_ = bf16[80,1280]{1,0:T(8,128)(2,1)S(1)} collective-permute-done((bf16[80,1280]{1,0:T(8,128)(2,1)S(1)}, bf16[80,1280]{1,0:T(8,128)(2,1)S(1)}, u32[]{:S(2)}, u32[]{:S(2)}) %collective-permute-start.20) | collective-permute-done | bytes 204832 | tf_op jit(solution)/shard_map/ppermute | solution.py:22
  (57 shorter events, 11.9 us)
Async XLA Ops:
  6.5 111.2 %all-gather.2.cloned.1.call-start = ((), (), s32[]{:S(2)}) async-start(), calls=%async_computation.3 | async-start | bytes 4423680 | tf_op jit(solution)/shard_map/all_gather | solution.py:285
  45.3 22.9 %collective-permute-start = (bf16[8,6,80,128]{3,2,1,0:T(8,128)(2,1)S(1)}, bf16[8,6,80,128]{3,2,1,0:T(8,128)(2,1)S(1)}, u32[]{:S(2)}, u32[]{:S(2)}) collective-permute-start(bf16[8,6,80,128]{3,2,1,0:T(8,128)(2,1)S(1)} %all_to_all.15.refs_0_), channel_id=1, source_target_pairs={{0,32},{32,64},{64,96},{96,0},{1,33},{33,65},{65,97},{97,1},{2,34}... | collective-permute-start | bytes 2949128 | tf_op jit(solution)/shard_map/ppermute | solution.py:22
  46.9 22.5 %collective-permute-start.1 = (bf16[8,6,80,128]{3,2,1,0:T(8,128)(2,1)S(1)}, bf16[8,6,80,128]{3,2,1,0:T(8,128)(2,1)}, u32[]{:S(2)}, u32[]{:S(2)}) collective-permute-start(bf16[8,6,80,128]{3,2,1,0:T(8,128)(2,1)S(1)} %all_to_all.15.refs_0_), channel_id=1, source_target_pairs={{0,96},{32,0},{64,32},{96,64},{1,97},{33,1},{65,33},{97,65},{2,98}... | collective-permute-start | bytes 2949128 | tf_op jit(solution)/shard_map/ppermute | solution.py:22
  48.7 26.3 %collective-permute-start.3 = (bf16[8,6,80,128]{3,2,1,0:T(8,128)(2,1)S(1)}, bf16[8,6,80,128]{3,2,1,0:T(8,128)(2,1)S(1)}, u32[]{:S(2)}, u32[]{:S(2)}) collective-permute-start(bf16[8,6,80,128]{3,2,1,0:T(8,128)(2,1)S(1)} %all_to_all.15.refs_0_), channel_id=1, source_target_pairs={{0,8},{8,0},{1,9},{9,1},{2,10},{10,2},{3,11},{11,3},{4,12},{12,4},... | collective-permute-start | bytes 2949128 | tf_op jit(solution)/shard_map/ppermute | solution.py:22
  48.7 26.2 %all-to-all-start.1 = ((bf16[8,3,80,128]{3,2,1,0:T(8,128)(2,1)}), bf16[8,3,80,128]{3,2,1,0:T(8,128)(2,1)S(1)}, u32[]{:S(2)}, u32[]{:S(2)}) async-start(bf16[8,3,80,128]{3,2,1,0:T(8,128)(2,1)} %get-tuple-element.20), calls=%async_computation.1 | async-start | bytes 983040 | tf_op jit(solution)/shard_map/all_to_all | solution.py:287
  69.1 11.8 %collective-permute-start.6 = (bf16[4,6,80,128]{3,2,1,0:T(8,128)(2,1)}, bf16[4,6,80,128]{3,2,1,0:T(8,128)(2,1)}, u32[]{:S(2)}, u32[]{:S(2)}) collective-permute-start(bf16[4,6,80,128]{3,2,1,0:T(8,128)(2,1)} %slice.16), channel_id=1, source_target_pairs={{0,32},{32,64},{64,96},{96,0},{1,33},{33,65},{65,97},{97,1},{2,34}... | collective-permute-start | bytes 1474568 | tf_op jit(solution)/shard_map/ppermute | solution.py:22
  71.3 10.8 %collective-permute-start.7 = (bf16[4,6,80,128]{3,2,1,0:T(8,128)(2,1)}, bf16[4,6,80,128]{3,2,1,0:T(8,128)(2,1)}, u32[]{:S(2)}, u32[]{:S(2)}) collective-permute-start(bf16[4,6,80,128]{3,2,1,0:T(8,128)(2,1)} %slice.17), channel_id=1, source_target_pairs={{0,96},{32,0},{64,32},{96,64},{1,97},{33,1},{65,33},{97,65},{2,98}... | collective-permute-start | bytes 1474568 | tf_op jit(solution)/shard_map/ppermute | solution.py:22
  74.2 13.9 %collective-permute-start.4 = (bf16[8,6,80,128]{3,2,1,0:T(8,128)(2,1)S(1)}, bf16[8,6,80,128]{3,2,1,0:T(8,128)(2,1)}, u32[]{:S(2)}, u32[]{:S(2)}) collective-permute-start(bf16[8,6,80,128]{3,2,1,0:T(8,128)(2,1)S(1)} %collective-permute-done.refs_2_), channel_id=1, source_target_pairs={{0,8},{8,0},{1,9},{9,1},{2,10},{10,2},{3,11},{11,3},{4,12},{12,4},... | collective-permute-start | bytes 2949128 | tf_op jit(solution)/shard_map/ppermute | solution.py:22
  74.2 13.9 %collective-permute-start.5 = (bf16[8,6,80,128]{3,2,1,0:T(8,128)(2,1)}, bf16[8,6,80,128]{3,2,1,0:T(8,128)(2,1)}, u32[]{:S(2)}, u32[]{:S(2)}) collective-permute-start(bf16[8,6,80,128]{3,2,1,0:T(8,128)(2,1)} %collective-permute-done.1.refs_4_), channel_id=1, source_target_pairs={{0,8},{8,0},{1,9},{9,1},{2,10},{10,2},{3,11},{11,3},{4,12},{12,4},... | collective-permute-start | bytes 2949128 | tf_op jit(solution)/shard_map/ppermute | solution.py:22
  74.9 13.2 %collective-permute-start.2 = (bf16[8,3,80,128]{3,2,1,0:T(8,128)(2,1)S(1)}, bf16[8,3,80,128]{3,2,1,0:T(8,128)(2,1)S(1)}, u32[]{:S(2)}, u32[]{:S(2)}) collective-permute-start(bf16[8,3,80,128]{3,2,1,0:T(8,128)(2,1)S(1)} %all-to-all-done.1.q_ref), channel_id=1, source_target_pairs={{0,16},{16,0},{1,17},{17,1},{2,18},{18,2},{3,19},{19,3},{4,20},{20... | collective-permute-start | bytes 1474568 | tf_op jit(solution)/shard_map/ppermute | solution.py:22
  80.9 7.2 %collective-permute-start.8 = (bf16[4,6,80,128]{3,2,1,0:T(8,128)(2,1)}, bf16[4,6,80,128]{3,2,1,0:T(8,128)(2,1)S(1)}, u32[]{:S(2)}, u32[]{:S(2)}) collective-permute-start(bf16[4,6,80,128]{3,2,1,0:T(8,128)(2,1)} %collective-permute-done.6.refs_6_), channel_id=1, source_target_pairs={{0,8},{8,0},{1,9},{9,1},{2,10},{10,2},{3,11},{11,3},{4,12},{12,4},... | collective-permute-start | bytes 1474568 | tf_op jit(solution)/shard_map/ppermute | solution.py:22
  82.1 6.1 %collective-permute-start.9 = (bf16[4,6,80,128]{3,2,1,0:T(8,128)(2,1)}, bf16[4,6,80,128]{3,2,1,0:T(8,128)(2,1)S(1)}, u32[]{:S(2)}, u32[]{:S(2)}) collective-permute-start(bf16[4,6,80,128]{3,2,1,0:T(8,128)(2,1)} %collective-permute-done.7.refs_7_), channel_id=1, source_target_pairs={{0,8},{8,0},{1,9},{9,1},{2,10},{10,2},{3,11},{11,3},{4,12},{12,4},... | collective-permute-start | bytes 1474568 | tf_op jit(solution)/shard_map/ppermute | solution.py:22
  101.8 15.2 %collective-permute-start.10 = (bf16[3,672,128]{2,1,0:T(8,128)(2,1)S(1)}, bf16[3,672,128]{2,1,0:T(8,128)(2,1)S(1)}, u32[]{:S(2)}, u32[]{:S(2)}) collective-permute-start(bf16[3,672,128]{2,1,0:T(8,128)(2,1)S(1)} %shard_map.47), channel_id=1, source_target_pairs={{0,16},{16,0},{1,17},{17,1},{2,18},{18,2},{3,19},{19,3},{4,20},{20... | collective-permute-start | bytes 1548296 | tf_op jit(solution)/shard_map/ppermute | solution.py:22
  117.8 37.1 %collective-permute-start.15 = (bf16[3072,640]{1,0:T(8,128)(2,1)}, bf16[3072,640]{1,0:T(8,128)(2,1)S(1)}, u32[]{:S(2)}, u32[]{:S(2)}) collective-permute-start(bf16[3072,640]{1,0:T(8,128)(2,1)} %all-gather.2.cloned.1.call-done.refs_6_.refs_2_), channel_id=1, source_target_pairs={{0,8},{8,0},{1,9},{9,1},{2,10},{10,2},{3,11},{11,3},{4,12},{12,4},... | collective-permute-start | bytes 11796488 | tf_op jit(solution)/shard_map/ppermute | solution.py:22
  138.2 8.9 %collective-permute-start.14 = (bf16[4,3,80,128]{3,2,1,0:T(8,128)(2,1)S(1)}, bf16[4,3,80,128]{3,2,1,0:T(8,128)(2,1)S(1)}, u32[]{:S(2)}, u32[]{:S(2)}) collective-permute-start(bf16[4,3,80,128]{3,2,1,0:T(8,128)(2,1)S(1)} %get-tuple-element.31), channel_id=1, source_target_pairs={{0,96},{32,0},{64,32},{96,64},{1,97},{33,1},{65,33},{97,65},{2,98}... | collective-permute-start | bytes 737288 | tf_op jit(solution)/shard_map/ppermute | solution.py:22
  139.5 10.1 %collective-permute-start.11 = (bf16[4,3,80,128]{3,2,1,0:T(8,128)(2,1)S(1)}, bf16[4,3,80,128]{3,2,1,0:T(8,128)(2,1)S(1)}, u32[]{:S(2)}, u32[]{:S(2)}) collective-permute-start(bf16[4,3,80,128]{3,2,1,0:T(8,128)(2,1)S(1)} %get-tuple-element.32), channel_id=1, source_target_pairs={{0,32},{32,64},{64,96},{96,0},{1,33},{33,65},{65,97},{97,1},{2,34}... | collective-permute-start | bytes 737288 | tf_op jit(solution)/shard_map/ppermute | solution.py:22
  140.3 12.1 %collective-permute-start.12 = (bf16[4,3,80,128]{3,2,1,0:T(8,128)(2,1)S(1)}, bf16[4,3,80,128]{3,2,1,0:T(8,128)(2,1)S(1)}, u32[]{:S(2)}, u32[]{:S(2)}) collective-permute-start(bf16[4,3,80,128]{3,2,1,0:T(8,128)(2,1)S(1)} %get-tuple-element.32), channel_id=1, source_target_pairs={{0,96},{32,0},{64,32},{96,64},{1,97},{33,1},{65,33},{97,65},{2,98}... | collective-permute-start | bytes 737288 | tf_op jit(solution)/shard_map/ppermute | solution.py:22
  142.8 12.1 %collective-permute-start.13 = (bf16[4,3,80,128]{3,2,1,0:T(8,128)(2,1)S(1)}, bf16[4,3,80,128]{3,2,1,0:T(8,128)(2,1)S(1)}, u32[]{:S(2)}, u32[]{:S(2)}) collective-permute-start(bf16[4,3,80,128]{3,2,1,0:T(8,128)(2,1)S(1)} %get-tuple-element.31), channel_id=1, source_target_pairs={{0,32},{32,64},{64,96},{96,0},{1,33},{33,65},{65,97},{97,1},{2,34}... | collective-permute-start | bytes 737288 | tf_op jit(solution)/shard_map/ppermute | solution.py:22
  147.1 18.1 %collective-permute-start.18 = (bf16[4,3,80,128]{3,2,1,0:T(8,128)(2,1)S(1)}, bf16[4,3,80,128]{3,2,1,0:T(8,128)(2,1)S(1)}, u32[]{:S(2)}, u32[]{:S(2)}) collective-permute-start(bf16[4,3,80,128]{3,2,1,0:T(8,128)(2,1)S(1)} %collective-permute-done.14.refs_5_), channel_id=1, source_target_pairs={{0,96},{32,0},{64,32},{96,64},{1,97},{33,1},{65,33},{97,65},{2,98}... | collective-permute-start | bytes 737288 | tf_op jit(solution)/shard_map/ppermute | solution.py:22
  149.6 15.7 %collective-permute-start.17 = (bf16[4,3,80,128]{3,2,1,0:T(8,128)(2,1)S(1)}, bf16[4,3,80,128]{3,2,1,0:T(8,128)(2,1)S(1)}, u32[]{:S(2)}, u32[]{:S(2)}) collective-permute-start(bf16[4,3,80,128]{3,2,1,0:T(8,128)(2,1)S(1)} %collective-permute-done.11.refs_1_), channel_id=1, source_target_pairs={{0,32},{32,64},{64,96},{96,0},{1,33},{33,65},{65,97},{97,1},{2,34}... | collective-permute-start | bytes 737288 | tf_op jit(solution)/shard_map/ppermute | solution.py:22
  165.3 18.2 %copy-start = (bf16[80,1280]{1,0:T(8,128)(2,1)S(1)}, bf16[80,1280]{1,0:T(8,128)(2,1)}, u32[]{:S(2)}) copy-start(bf16[80,1280]{1,0:T(8,128)(2,1)} %get-tuple-element.26.refs_0_) | copy-start | bytes 614404
  172.7 8.6 %collective-permute-start.19 = (bf16[80,1280]{1,0:T(8,128)(2,1)}, bf16[80,1280]{1,0:T(8,128)(2,1)S(1)}, u32[]{:S(2)}, u32[]{:S(2)}) collective-permute-start(bf16[80,1280]{1,0:T(8,128)(2,1)} %shard_map.51), channel_id=1, source_target_pairs={{0,64},{32,96},{64,0},{96,32},{1,65},{33,97},{65,1},{97,33},{2,66}... | collective-permute-start | bytes 614408 | tf_op jit(solution)/shard_map/ppermute | solution.py:22
  172.7 8.8 %collective-permute-start.16 = (bf16[80,1280]{1,0:T(8,128)(2,1)S(1)}, bf16[80,1280]{1,0:T(8,128)(2,1)S(1)}, u32[]{:S(2)}, u32[]{:S(2)}) collective-permute-start(bf16[80,1280]{1,0:T(8,128)(2,1)S(1)} %copy-done.10), channel_id=1, source_target_pairs={{0,96},{32,0},{64,32},{96,64},{1,97},{33,1},{65,33},{97,65},{2,98}... | collective-permute-start | bytes 614408 | tf_op jit(solution)/shard_map/ppermute | solution.py:22
  175.0 8.5 %collective-permute-start.20 = (bf16[80,1280]{1,0:T(8,128)(2,1)S(1)}, bf16[80,1280]{1,0:T(8,128)(2,1)S(1)}, u32[]{:S(2)}, u32[]{:S(2)}) collective-permute-start(bf16[80,1280]{1,0:T(8,128)(2,1)S(1)} %copy-done.9), channel_id=1, source_target_pairs={{0,32},{32,64},{64,96},{96,0},{1,33},{33,65},{65,97},{97,1},{2,34}... | collective-permute-start | bytes 614408 | tf_op jit(solution)/shard_map/ppermute | solution.py:22
  (10 other events, 53.4 us)
Sparse Core Ops, SparseCore 0:
  45.5 59.0 all-gather.1
